TPU v7x, 32 devices: a whole 2x2x4 slice. The times are simulated.
32 devices in a mesh: prow: 8 (over y, x, core), pcol: 4 (over z).
Axes of the slice: x: 2, y: 2, z: 4, core: 2. Of those that a mesh axis runs over, the one named last changes fastest.
Arguments:
- anc_inverse: bfloat16 [2, 2, 8, 256, 4, 4, 256], P(None, None, 'prow', None, None, 'pcol'), may hold values from -6 to 6
- factor_panel: bfloat16 [2, 2, 8, 256, 4, 4, 256], P(None, None, 'prow', None, None, 'pcol'), may hold values from -0.09375 to 0.09375
- diag_inverse: bfloat16 [2, 4, 4, 256, 2, 8, 256], P(None, None, 'pcol', None, None, 'prow'), may hold values from -6 to 6
- block_pattern: int32 [2, 16, 16], replicated, may hold values from 0 to 1, as said below
Outputs:
- sigma_off: bfloat16 [2, 2, 8, 256, 4, 4, 256], P(None, None, 'prow', None, None, 'pcol')
- sigma_diag: bfloat16 [2, 4, 4, 256, 2, 8, 256], P(None, None, 'pcol', None, None, 'prow')
Inputs may be any that keep to these rules, and one draw needn't show every extreme that they name: `block_pattern`: symmetric in its last two dimensions, with ones on the diagonal.
All inputs are finite; a program needn't handle non-finite values.
Results may differ from a plain program's by a relative error of at most 0.0039.
Values may be sent and summed in bfloat16 or wider, within the bound.
A program may use at most 128 MiB of HBM per device.

v0:
```python
import jax
import jax.numpy as jnp
from jax import lax
from jax.sharding import PartitionSpec as P


def invert_window(anc_local, panel_local, diag_local, owned_rows, col_index):
    nodes_here = anc_local.shape[0]
    width_blk = anc_local.shape[3]
    cols_loc = anc_local.shape[4]
    panel_cols = panel_local.shape[4]
    col_devices = lax.axis_size("pcol")
    row_devices = lax.axis_size("prow")
    own_mask = lax.dynamic_slice_in_dim(owned_rows, col_index, 1, 4)
    keep_mask = own_mask[:, :, :, None, :, :, None] != 0
    masked = jnp.where(keep_mask, anc_local, jnp.zeros_like(anc_local))
    gathered = lax.all_gather(panel_local, "prow", axis=2, tiled=True)
    by_owner = gathered.reshape(
        nodes_here, cols_loc, col_devices, width_blk, panel_cols, 1, width_blk
    )
    owner_panel = lax.all_to_all(by_owner, "pcol", split_axis=2, concat_axis=5, tiled=True)
    partial_terms = jnp.einsum(
        "sraicbj,scbjwnm->sraiwnm", masked, owner_panel, preferred_element_type=jnp.float32
    )
    product = lax.psum_scatter(partial_terms, "pcol", scatter_dimension=5, tiled=True)
    sigma_off = (-product).astype(jnp.bfloat16)
    all_cols = lax.all_gather(sigma_off, "pcol", axis=5, tiled=True)
    inner_sum = jnp.einsum(
        "sraiwbm,sraivnk->swbmvnk", panel_local, all_cols, preferred_element_type=jnp.float32
    )
    inner_sum = inner_sum.reshape(
        nodes_here,
        panel_cols,
        1,
        width_blk,
        panel_cols * col_devices // row_devices,
        row_devices,
        width_blk,
    )
    summed = lax.psum_scatter(inner_sum, "prow", scatter_dimension=5, tiled=True)
    sigma_diag = (diag_local.astype(jnp.float32) - summed).astype(jnp.bfloat16)
    return (sigma_off, sigma_diag)


def on_device(anc_inverse, factor_panel, diag_inverse, block_pattern):
    row_index = lax.axis_index("prow")
    col_index = lax.axis_index("pcol")
    row_devices = lax.axis_size("prow")
    col_devices = lax.axis_size("pcol")
    nodes_all = anc_inverse.shape[0]
    pattern_grid = block_pattern.reshape(
        nodes_all, anc_inverse.shape[1], row_devices, anc_inverse.shape[4], col_devices
    )
    owned_rows = lax.dynamic_slice_in_dim(pattern_grid, row_index, 1, 2)
    off_list = []
    diag_list = []
    for supernode in range(nodes_all):
        off_block, diag_block = invert_window(
            anc_inverse[supernode : supernode + 1],
            factor_panel[supernode : supernode + 1],
            diag_inverse[supernode : supernode + 1],
            owned_rows[supernode : supernode + 1],
            col_index,
        )
        off_list.append(off_block)
        diag_list.append(diag_block)
    return (jnp.concatenate(off_list, axis=0), jnp.concatenate(diag_list, axis=0))


def solution(mesh):
    return jax.shard_map(
        on_device,
        mesh=mesh,
        in_specs=(
            P(None, None, "prow", None, None, "pcol", None),
            P(None, None, "prow", None, None, "pcol", None),
            P(None, None, "pcol", None, None, "prow", None),
            P(),
        ),
        out_specs=(
            P(None, None, "prow", None, None, "pcol", None),
            P(None, None, "pcol", None, None, "prow", None),
        ),
        check_vma=False,
    )
```

profile of v0, /device:TPU:7, one launch (start us, length us, event | category | flops | bytes accessed | tf_op | source)
XLA Modules:
  0.0 1635.2 jit_solution(18038620402629778326)
XLA Ops:
  11.8 54.0 %all-gather.5.cloned.1.call-done = bf16[1,2,8,256,4,1,256]{6,3,5,4,1,0,2:T(8,128)(2,1)} async-done(((bf16[1,2,1,256,4,1,256]{6,3,5,4,1,0,2:T(8,128)(2,1)}), bf16[1,2,8,256,4,1,256]{6,3,5,4,1,0,2:T(8,128)(2,1)}) %all-gather.5.cloned.1.call-update) | async-done | bytes 8388624 | tf_op jit(solution)/shard_map/all_gather | solution.py:17
  65.8 7.6 copy.59
  73.5 8.0 copy.60
  81.4 5.7 all-to-all-start
  87.1 35.6 %all-gather.7.cloned.1.call-done = bf16[1,2,8,256,4,1,256]{6,3,5,4,1,0,2:T(8,128)(2,1)} async-done(((bf16[1,2,1,256,4,1,256]{6,3,5,4,1,0,2:T(8,128)(2,1)}), bf16[1,2,8,256,4,1,256]{6,3,5,4,1,0,2:T(8,128)(2,1)}) %all-gather.7.cloned.1.call-update) | async-done | bytes 8388624 | tf_op jit(solution)/shard_map/all_gather | solution.py:17
  122.7 7.6 copy.65
  130.3 7.6 copy.66
  138.0 132.1 %all-to-all-done = bf16[1,4,4,256,4,1,256]{6,3,1,4,5,0,2:T(8,128)(2,1)} async-done(((bf16[1,4,4,256,4,1,256]{6,3,1,4,5,0,2:T(8,128)(2,1)}), bf16[1,4,4,256,4,1,256]{6,3,1,4,5,0,2:T(8,128)(2,1)}, u32[]{:S(2)}, u32[]{:S(2)}) %all-to-all-start) | async-done | bytes 8388640 | tf_op jit(solution)/shard_map/all_to_all | solution.py:21
  270.1 5.6 all-to-all-start.1
  278.7 10.1 fusion.6
  288.7 169.5 %all-to-all-done.1 = bf16[1,4,4,256,4,1,256]{6,3,1,4,5,0,2:T(8,128)(2,1)} async-done(((bf16[1,4,4,256,4,1,256]{6,3,1,4,5,0,2:T(8,128)(2,1)}), bf16[1,4,4,256,4,1,256]{6,3,1,4,5,0,2:T(8,128)(2,1)}, u32[]{:S(2)}, u32[]{:S(2)}) %all-to-all-start.1) | async-done | bytes 8388640 | tf_op jit(solution)/shard_map/all_to_all | solution.py:21
  458.3 10.1 fusion.9
  469.6 562.4 %all-reduce.11.cloned.1.call-done = (f32[1,2,1,256,4,4,256]{6,3,5,4,1,2,0:T(8,128)}, f32[1,2,1,256,4,4,256]{6,3,5,4,1,2,0:T(8,128)}) async-done(((f32[1,2,1,256,4,4,256]{6,3,5,4,1,2,0:T(8,128)}, f32[1,2,1,256,4,4,256]{6,3,5,4,1,2,0:T(8,128)}), (f32[1,2,1,256,4,4,256]{6,3,5,4,1,2,0:T(8,128)}, f32[1,2,1,256,4,4,256]{6,3,5,4,1,2,0:T(8,128)})) %all-reduce.11.cloned.1.call-update) | async-done | bytes 16777232
  1032.0 3.4 fusion.14
  1035.4 3.4 fusion.15
  1040.4 74.8 %all-gather.11.cloned.1.call-done = bf16[1,2,1,256,4,4,256]{6,3,5,4,1,2,0:T(8,128)(2,1)} async-done(((bf16[1,2,1,256,4,1,256]{6,3,5,4,1,2,0:T(8,128)(2,1)}), bf16[1,2,1,256,4,4,256]{6,3,5,4,1,2,0:T(8,128)(2,1)}) %all-gather.11.cloned.1.call-update) | async-done | bytes 4194320 | tf_op jit(solution)/shard_map/all_gather | solution.py:27
  1115.3 7.3 copy.72
  1122.5 74.0 %all-gather.9.cloned.1.call-done = bf16[1,2,1,256,4,4,256]{6,3,5,4,1,2,0:T(8,128)(2,1)} async-done(((bf16[1,2,1,256,4,1,256]{6,3,5,4,1,2,0:T(8,128)(2,1)}), bf16[1,2,1,256,4,4,256]{6,3,5,4,1,2,0:T(8,128)(2,1)}) %all-gather.9.cloned.1.call-update) | async-done | bytes 4194320 | tf_op jit(solution)/shard_map/all_gather | solution.py:27
  1196.6 7.3 copy.70
  1203.9 10.5 convolution_bitcast_fusion
  1214.4 8.3 convolution_bitcast_fusion.1
  1223.9 3.6 fusion.20
  1235.1 384.3 %all-reduce.9.cloned.1.call-done = (f32[1,4,1,256,2,8,256]{3,6,1,5,4,2,0:T(8,128)}, f32[1,4,1,256,2,8,256]{3,6,1,5,4,2,0:T(8,128)}) async-done(((f32[1,4,1,256,2,8,256]{3,6,1,5,4,2,0:T(8,128)}, f32[1,4,1,256,2,8,256]{3,6,1,5,4,2,0:T(8,128)}), (f32[1,4,1,256,2,8,256]{3,6,1,5,4,2,0:T(8,128)}, f32[1,4,1,256,2,8,256]{3,6,1,5,4,2,0:T(8,128)})) %all-reduce.9.cloned.1.call-update) | async-done | bytes 33554448
  1624.6 3.8 copy.74
  (47 shorter events, 24.3 us)
Async XLA Ops:
  7.2 58.7 %all-gather.5.cloned.1.call-start = ((), (), s32[]{:S(2)}) async-start(), calls=%async_computation.2 | async-start | bytes 9437184 | tf_op jit(solution)/shard_map/all_gather | solution.py:17
  10.6 112.1 %all-gather.7.cloned.1.call-start = ((), (), s32[]{:S(2)}) async-start(), calls=%async_computation.3 | async-start | bytes 9437184 | tf_op jit(solution)/shard_map/all_gather | solution.py:17
  81.4 188.7 %all-to-all-start = ((bf16[1,4,4,256,4,1,256]{6,3,1,4,5,0,2:T(8,128)(2,1)}), bf16[1,4,4,256,4,1,256]{6,3,1,4,5,0,2:T(8,128)(2,1)}, u32[]{:S(2)}, u32[]{:S(2)}) async-start(bf16[1,4,4,256,4,1,256]{6,3,1,4,5,0,2:T(8,128)(2,1)} %copy.60), calls=%async_computation | async-start | bytes 16777216 | tf_op jit(solution)/shard_map/all_to_all | solution.py:21
  138.0 137.8 %copy-start.4 = (s32[2,16,16]{2,1,0:T(8,128)S(1)}, s32[2,16,16]{2,1,0:T(8,128)}, u32[]{:S(2)}) copy-start(s32[2,16,16]{2,1,0:T(8,128)} %param.7) | copy-start | bytes 6148
  270.1 188.2 %all-to-all-start.1 = ((bf16[1,4,4,256,4,1,256]{6,3,1,4,5,0,2:T(8,128)(2,1)}), bf16[1,4,4,256,4,1,256]{6,3,1,4,5,0,2:T(8,128)(2,1)}, u32[]{:S(2)}, u32[]{:S(2)}) async-start(bf16[1,4,4,256,4,1,256]{6,3,1,4,5,0,2:T(8,128)(2,1)} %copy.66), calls=%async_computation.1 | async-start | bytes 16777216 | tf_op jit(solution)/shard_map/all_to_all | solution.py:21
  275.7 756.3 %all-reduce.11.cloned.1.call-start = ((), (), s32[]{:S(2)}) async-start(), calls=%async_computation.7 | async-start | bytes 33554432
  468.3 0.7 copy-start.6
  468.4 646.9 %all-gather.11.cloned.1.call-start = ((), (), s32[]{:S(2)}) async-start(), calls=%async_computation.5 | async-start | bytes 5242880 | tf_op jit(solution)/shard_map/all_gather | solution.py:27
  1035.4 161.2 %all-gather.9.cloned.1.call-start = ((), (), s32[]{:S(2)}) async-start(), calls=%async_computation.4 | async-start | bytes 5242880 | tf_op jit(solution)/shard_map/all_gather | solution.py:27
  1038.8 580.6 %all-reduce.9.cloned.1.call-start = ((), (), s32[]{:S(2)}) async-start(), calls=%async_computation.6 | async-start | bytes 67108864
  1203.9 10.5 copy-start.3
  1222.7 0.7 copy-start.5
  1223.9 8.0 copy-start
  1223.9 8.0 copy-start.1
  1232.2 387.3 %copy-start.2 = (bf16[1,4,1,256,2,1,256]{3,6,1,5,4,2,0:T(8,128)(2,1)S(1)}, bf16[1,4,1,256,2,1,256]{3,6,1,5,4,2,0:T(8,128)(2,1)}, u32[]{:S(2)}) copy-start(bf16[1,4,1,256,2,1,256]{3,6,1,5,4,2,0:T(8,128)(2,1)} %copy.104) | copy-start | bytes 3145732
Sparse Core Ops, SparseCore 0:
  10.7 55.0 all-gather.4
  68.3 54.3 all-gather.6
  468.5 563.4 all-reduce.10
  1035.5 79.7 all-gather.10
  1117.2 79.2 all-gather.8
  1222.8 396.5 all-reduce.8
where the time goes:
time: 1640 us
  waiting for transfers between devices  1490 us (91%)
  local copies, waits for them, and re-layouts  68.8 us (4%)
  matrix products  38.9 us (2%)
    unnamed x8, waiting for transfers between devices  947 us
    all_to_all x2, waiting for transfers between devices, invert_window(): lax.all_to_all(by_owner, 'pcol', split_axis=2, concat_axis=5, tiled=True)  302 us
    all_gather x2, waiting for transfers between devices, invert_window(): all_cols = lax.all_gather(sigma_off, 'pcol', axis=5, tiled=True)  149 us
    all_gather x2, waiting for transfers between devices, invert_window(): gathered = lax.all_gather(panel_local, 'prow', axis=2, tiled=True)  89.7 us
  transfers between devices with their start and end apart: 8, of which 8 were waited for; matrix products, arithmetic and copies ran while one was open for 4% of the time, Pallas kernels for 0%

commit v1 on v0

--- a/solution.py
+++ b/solution.py
@@ -5,40 +5,32 @@
 
 
 def invert_window(anc_local, panel_local, diag_local, owned_rows, col_index):
-    nodes_here = anc_local.shape[0]
-    width_blk = anc_local.shape[3]
-    cols_loc = anc_local.shape[4]
+    nodes_here, rows_loc, _, width_blk, cols_loc, _, _ = anc_local.shape
     panel_cols = panel_local.shape[4]
     col_devices = lax.axis_size("pcol")
     row_devices = lax.axis_size("prow")
+    diag_cols = diag_local.shape[4]
     own_mask = lax.dynamic_slice_in_dim(owned_rows, col_index, 1, 4)
     keep_mask = own_mask[:, :, :, None, :, :, None] != 0
     masked = jnp.where(keep_mask, anc_local, jnp.zeros_like(anc_local))
-    gathered = lax.all_gather(panel_local, "prow", axis=2, tiled=True)
-    by_owner = gathered.reshape(
-        nodes_here, cols_loc, col_devices, width_blk, panel_cols, 1, width_blk
+    masked_all = lax.all_gather(masked, "pcol", axis=5, tiled=True)
+    panel_all = lax.all_gather(panel_local, "prow", axis=2, tiled=True)
+    panel_rows = panel_all.reshape(
+        nodes_here, cols_loc, col_devices, width_blk, panel_cols, width_blk
     )
-    owner_panel = lax.all_to_all(by_owner, "pcol", split_axis=2, concat_axis=5, tiled=True)
-    partial_terms = jnp.einsum(
-        "sraicbj,scbjwnm->sraiwnm", masked, owner_panel, preferred_element_type=jnp.float32
+    product = jnp.einsum(
+        "sraicbj,scbjwm->sraiwm", masked_all, panel_rows, preferred_element_type=jnp.float32
     )
-    product = lax.psum_scatter(partial_terms, "pcol", scatter_dimension=5, tiled=True)
-    sigma_off = (-product).astype(jnp.bfloat16)
+    sigma_off = (-product).astype(jnp.bfloat16)[:, :, :, :, :, None, :]
     all_cols = lax.all_gather(sigma_off, "pcol", axis=5, tiled=True)
+    by_owner = all_cols.reshape(
+        nodes_here, rows_loc, 1, width_blk, diag_cols, row_devices, width_blk
+    )
+    own_cols = lax.all_to_all(by_owner, "prow", split_axis=5, concat_axis=2, tiled=True)
     inner_sum = jnp.einsum(
-        "sraiwbm,sraivnk->swbmvnk", panel_local, all_cols, preferred_element_type=jnp.float32
+        "sraiwbm,sraivnk->swbmvnk", panel_all, own_cols, preferred_element_type=jnp.float32
     )
-    inner_sum = inner_sum.reshape(
-        nodes_here,
-        panel_cols,
-        1,
-        width_blk,
-        panel_cols * col_devices // row_devices,
-        row_devices,
-        width_blk,
-    )
-    summed = lax.psum_scatter(inner_sum, "prow", scatter_dimension=5, tiled=True)
-    sigma_diag = (diag_local.astype(jnp.float32) - summed).astype(jnp.bfloat16)
+    sigma_diag = (diag_local.astype(jnp.float32) - inner_sum).astype(jnp.bfloat16)
     return (sigma_off, sigma_diag)
 
 

time: 1640 us -> 535 us (0.33)
  waiting for transfers between devices: 1490 us -> 404 us
    unnamed x8 -> x6, waiting for transfers between devices: 947 us -> 0.1 us
    all_to_all x2, waiting for transfers between devices: 302 us -> 24.8 us  [invert_window(): lax.all_to_all(by_owner, 'prow', split_axis=5, concat_axis=2, tiled=True)]
    all_gather x2 -> x4, waiting for transfers between devices: 89.7 us -> 244 us  [the longest x2 151 us: invert_window(): masked_all = lax.all_gather(masked, 'pcol', axis=5, tiled=True)]
  transfers between devices with their start and end apart: 8 -> 8, of which waited for: 8 -> 7; matrix products, arithmetic and copies ran while one was open for 4% -> 16% of each run, Pallas kernels for 0% -> 0%
where the time goes in v1:
time: 535 us; the launch traced here: 531 us
  waiting for transfers between devices  404 us (76%)
  local copies, waits for them, and re-layouts  60.5 us (11%)
  matrix products  38.6 us (7%)
  between operations  14.2 us (3%)
  starting transfers between devices  10.6 us (2%)
    all_gather x2, waiting for transfers between devices, invert_window(): masked_all = lax.all_gather(masked, 'pcol', axis=5, tiled=True)  151 us
    all_gather x2, waiting for transfers between devices, invert_window(): all_cols = lax.all_gather(sigma_off, 'pcol', axis=5, tiled=True)  135 us
    all_gather x2, waiting for transfers between devices, invert_window(): panel_all = lax.all_gather(panel_local, 'prow', axis=2, tiled=True)  93.5 us
    all_to_all x2, waiting for transfers between devices, invert_window(): lax.all_to_all(by_owner, 'prow', split_axis=5, concat_axis=2, tiled=True)  24.8 us
    dot_general x2, matrix products, invert_window(): jnp.einsum('sraicbj,scbjwm->sraiwm', masked_all, panel_rows, preferred_el...  20.3 us
    dot_general x2, matrix products, invert_window(): jnp.einsum('sraiwbm,sraivnk->swbmvnk', panel_all, own_cols, preferred_ele...  18.4 us
    all_gather x2, local copies, waits for them, and re-layouts, invert_window(): panel_all = lax.all_gather(panel_local, 'prow', axis=2, tiled=True)  15.3 us
    unnamed x19, local copies, waits for them, and re-layouts  14.9 us
  transfers between devices with their start and end apart: 8, of which 7 were waited for; matrix products, arithmetic and copies ran while one was open for 16% of the time, Pallas kernels for 0%

profile of v1, /device:TPU:7, one launch (start us, length us, event | category | flops | bytes accessed | tf_op | source)
XLA Modules:
  0.0 530.9 jit_solution(1460207585947471451)
XLA Ops:
  11.1 2.3 fusion.37
  17.0 48.8 %all-gather.11.cloned.1.call-done = bf16[1,2,8,256,4,1,256]{6,3,1,2,4,5,0:T(8,128)(2,1)} async-done(((bf16[1,2,1,256,4,1,256]{6,3,1,2,4,5,0:T(8,128)(2,1)}), bf16[1,2,8,256,4,1,256]{6,3,1,2,4,5,0:T(8,128)(2,1)}) %all-gather.11.cloned.1.call-update) | async-done | bytes 8388624 | tf_op jit(solution)/shard_map/all_gather | solution.py:17
  65.9 7.6 %copy.59 = bf16[1,2,8,256,4,1,256]{6,3,5,4,2,1,0:T(8,128)(2,1)} copy(bf16[1,2,8,256,4,1,256]{6,3,1,2,4,5,0:T(8,128)(2,1)} %all-gather.11.cloned.1.call-done) | data formatting | bytes 16777216 | tf_op jit(solution)/shard_map/all_gather | solution.py:17
  73.5 75.2 %all-gather.9.cloned.1.call-done = bf16[1,2,1,256,4,4,256]{6,3,4,5,1,2,0:T(8,128)(2,1)} async-done(((bf16[1,2,1,256,4,1,256]{6,3,4,5,1,2,0:T(8,128)(2,1)}), bf16[1,2,1,256,4,4,256]{6,3,4,5,1,2,0:T(8,128)(2,1)}) %all-gather.9.cloned.1.call-update) | async-done | bytes 4194320 | tf_op jit(solution)/shard_map/all_gather | solution.py:16
  148.7 10.1 %fusion.19 = bf16[2,256,4,256]{3,1,2,0:T(8,128)(2,1)} fusion(bf16[4,4,256,4,256]{4,2,3,1,0:T(8,128)(2,1)} %bitcast.114, bf16[1,2,1,256,4,4,256]{6,3,4,5,1,2,0:T(8,128)(2,1)} %all-gather.9.cloned.1.call-done), kind=kOutput, calls=%fused_computation.25 | convolution fusion | flops 4296015872 | bytes 13631488 | tf_op jit(solution)/shard_map/sraicbj,scbjwm->sraiwm/dot_general | solution.py:21
  159.0 44.7 %all-gather.15.cloned.1.call-done = bf16[1,2,8,256,4,1,256]{6,3,1,2,4,5,0:T(8,128)(2,1)} async-done(((bf16[1,2,1,256,4,1,256]{6,3,1,2,4,5,0:T(8,128)(2,1)}), bf16[1,2,8,256,4,1,256]{6,3,1,2,4,5,0:T(8,128)(2,1)}) %all-gather.15.cloned.1.call-update) | async-done | bytes 8388624 | tf_op jit(solution)/shard_map/all_gather | solution.py:17
  203.7 7.6 %copy.63 = bf16[1,2,8,256,4,1,256]{6,3,5,4,2,1,0:T(8,128)(2,1)} copy(bf16[1,2,8,256,4,1,256]{6,3,1,2,4,5,0:T(8,128)(2,1)} %all-gather.15.cloned.1.call-done) | data formatting | bytes 16777216 | tf_op jit(solution)/shard_map/all_gather | solution.py:17
  211.3 75.7 %all-gather.13.cloned.1.call-done = bf16[1,2,1,256,4,4,256]{6,3,4,5,1,2,0:T(8,128)(2,1)} async-done(((bf16[1,2,1,256,4,1,256]{6,3,4,5,1,2,0:T(8,128)(2,1)}), bf16[1,2,1,256,4,4,256]{6,3,4,5,1,2,0:T(8,128)(2,1)}) %all-gather.13.cloned.1.call-update) | async-done | bytes 4194320 | tf_op jit(solution)/shard_map/all_gather | solution.py:16
  287.0 10.1 %fusion.18 = bf16[2,256,4,256]{3,1,2,0:T(8,128)(2,1)} fusion(bf16[4,4,256,4,256]{4,2,3,1,0:T(8,128)(2,1)} %bitcast.115, bf16[1,2,1,256,4,4,256]{6,3,4,5,1,2,0:T(8,128)(2,1)} %all-gather.13.cloned.1.call-done), kind=kOutput, calls=%fused_computation.23 | convolution fusion | flops 4296015872 | bytes 13631488 | tf_op jit(solution)/shard_map/sraicbj,scbjwm->sraiwm/dot_general | solution.py:21
  297.1 70.6 %all-gather.17.cloned.1.call-done = bf16[2,256,4,1024]{3,1,2,0:T(8,128)(2,1)} async-done(((bf16[2,256,4,256]{3,1,2,0:T(8,128)(2,1)}), bf16[2,256,4,1024]{3,1,2,0:T(8,128)(2,1)}) %all-gather.17.cloned.1.call-update) | async-done | bytes 4194320 | tf_op jit(solution)/shard_map/all_gather | solution.py:25
  367.7 6.2 %copy.66 = bf16[2,256,4,1024]{1,3,2,0:T(8,128)(2,1)} copy(bf16[2,256,4,1024]{3,1,2,0:T(8,128)(2,1)} %all-gather.17.cloned.1.call-done) | data formatting | bytes 8388608 | tf_op jit(solution)/shard_map/all_gather | solution.py:25
  373.9 5.0 copy.67
  378.9 5.2 all-to-all-start
  384.1 64.4 %all-gather.19.cloned.1.call-done = bf16[2,256,4,1024]{3,1,2,0:T(8,128)(2,1)} async-done(((bf16[2,256,4,256]{3,1,2,0:T(8,128)(2,1)}), bf16[2,256,4,1024]{3,1,2,0:T(8,128)(2,1)}) %all-gather.19.cloned.1.call-update) | async-done | bytes 4194320 | tf_op jit(solution)/shard_map/all_gather | solution.py:25
  448.5 6.2 %copy.70 = bf16[2,256,4,1024]{1,3,2,0:T(8,128)(2,1)} copy(bf16[2,256,4,1024]{3,1,2,0:T(8,128)(2,1)} %all-gather.19.cloned.1.call-done) | data formatting | bytes 8388608 | tf_op jit(solution)/shard_map/all_gather | solution.py:25
  454.7 4.6 copy.71
  459.3 5.1 all-to-all-start.1
  464.5 3.6 fusion.36
  468.1 3.7 copy.92
  474.0 2.9 copy.73
  476.9 9.2 %fusion.17 = bf16[1,4,1,256,2,1,256]{3,6,1,4,5,2,0:T(8,128)(2,1)S(1)} fusion(bf16[1,4,1,256,2,1,256]{3,6,1,4,5,2,0:T(8,128)(2,1)S(1)} %copy-done.3, bf16[1,2,8,256,4,1,256]{6,3,1,2,4,5,0:T(8,128)(2,1)} %all-gather.11.cloned.1.call-done, bf16[1,2,1,256,2,8,256]{3,6,1,4,2,0,5:T(8,128)(2,1)} %all-to-all-done), kind=kOutput, calls=%fused_computation.21 | convolution fusion | flops 4296540160 | bytes 14680064 | tf_op jit(solution)/shard_map/sraiwbm,sraivnk->swbmvnk/dot_general | solution.py:30
  486.1 24.8 %all-to-all-done.1 = bf16[1,2,1,256,2,8,256]{3,6,1,4,2,0,5:T(8,128)(2,1)} async-done(((bf16[1,2,1,256,2,8,256]{3,6,1,4,2,0,5:T(8,128)(2,1)}), bf16[1,2,1,256,2,8,256]{3,6,1,4,2,0,5:T(8,128)(2,1)}, u32[]{:S(2)}, u32[]{:S(2)}) %all-to-all-start.1) | async-done | bytes 4194336 | tf_op jit(solution)/shard_map/all_to_all | solution.py:29
  511.0 9.1 %fusion.16 = bf16[1,4,1,256,2,1,256]{3,6,1,4,5,2,0:T(8,128)(2,1)S(1)} fusion(bf16[1,4,1,256,2,1,256]{3,6,1,4,5,2,0:T(8,128)(2,1)S(1)} %copy-done.2, bf16[1,2,8,256,4,1,256]{6,3,1,2,4,5,0:T(8,128)(2,1)} %all-gather.15.cloned.1.call-done, bf16[1,2,1,256,2,8,256]{3,6,1,4,2,0,5:T(8,128)(2,1)} %all-to-all-done.1), kind=kOutput, calls=%fused_computation.19 | convolution fusion | flops 4296540160 | bytes 14680064 | tf_op jit(solution)/shard_map/sraiwbm,sraivnk->swbmvnk/dot_general | solution.py:30
  520.3 3.8 copy.74
  (38 shorter events, 10.0 us)
Async XLA Ops:
  7.2 3.5 copy-start.4
  7.2 58.7 %all-gather.11.cloned.1.call-start = ((), (), s32[]{:S(2)}) async-start(), calls=%async_computation.3 | async-start | bytes 9437184 | tf_op jit(solution)/shard_map/all_gather | solution.py:17
  10.6 138.1 %all-gather.9.cloned.1.call-start = ((), (), s32[]{:S(2)}) async-start(), calls=%async_computation.2 | async-start | bytes 5242880 | tf_op jit(solution)/shard_map/all_gather | solution.py:16
  14.5 189.2 %all-gather.15.cloned.1.call-start = ((), (), s32[]{:S(2)}) async-start(), calls=%async_computation.5 | async-start | bytes 9437184 | tf_op jit(solution)/shard_map/all_gather | solution.py:17
  15.7 271.3 %all-gather.13.cloned.1.call-start = ((), (), s32[]{:S(2)}) async-start(), calls=%async_computation.4 | async-start | bytes 5242880 | tf_op jit(solution)/shard_map/all_gather | solution.py:16
  17.0 350.7 %all-gather.17.cloned.1.call-start = ((), (), s32[]{:S(2)}) async-start(), calls=%async_computation.6 | async-start | bytes 5242880 | tf_op jit(solution)/shard_map/all_gather | solution.py:25
  158.9 289.6 %all-gather.19.cloned.1.call-start = ((), (), s32[]{:S(2)}) async-start(), calls=%async_computation.7 | async-start | bytes 5242880 | tf_op jit(solution)/shard_map/all_gather | solution.py:25
  378.9 80.4 %all-to-all-start = ((bf16[1,2,1,256,2,8,256]{3,6,1,4,2,0,5:T(8,128)(2,1)}), bf16[1,2,1,256,2,8,256]{3,6,1,4,2,0,5:T(8,128)(2,1)}, u32[]{:S(2)}, u32[]{:S(2)}) async-start(bf16[1,2,1,256,2,8,256]{3,6,1,4,2,0,5:T(8,128)(2,1)} %copy.67), calls=%async_computation | async-start | bytes 8388608 | tf_op jit(solution)/shard_map/all_to_all | solution.py:29
  459.3 51.6 %all-to-all-start.1 = ((bf16[1,2,1,256,2,8,256]{3,6,1,4,2,0,5:T(8,128)(2,1)}), bf16[1,2,1,256,2,8,256]{3,6,1,4,2,0,5:T(8,128)(2,1)}, u32[]{:S(2)}, u32[]{:S(2)}) async-start(bf16[1,2,1,256,2,8,256]{3,6,1,4,2,0,5:T(8,128)(2,1)} %copy.71), calls=%async_computation.1 | async-start | bytes 8388608 | tf_op jit(solution)/shard_map/all_to_all | solution.py:29
  464.5 9.3 %copy-start = (bf16[2,256,4,256]{3,1,2,0:T(8,128)(2,1)S(1)}, bf16[2,256,4,256]{3,1,2,0:T(8,128)(2,1)}, u32[]{:S(2)}) copy-start(bf16[2,256,4,256]{3,1,2,0:T(8,128)(2,1)} %fusion.19) | copy-start | bytes 3145732
  464.5 9.3 %copy-start.1 = (bf16[2,256,4,256]{3,1,2,0:T(8,128)(2,1)S(1)}, bf16[2,256,4,256]{3,1,2,0:T(8,128)(2,1)}, u32[]{:S(2)}) copy-start(bf16[2,256,4,256]{3,1,2,0:T(8,128)(2,1)} %fusion.18) | copy-start | bytes 3145732
  473.8 3.1 copy-start.3
  476.9 34.1 %copy-start.2 = (bf16[1,4,1,256,2,1,256]{3,6,1,4,5,2,0:T(8,128)(2,1)S(1)}, bf16[1,4,1,256,2,1,256]{3,6,1,4,5,2,0:T(8,128)(2,1)}, u32[]{:S(2)}) copy-start(bf16[1,4,1,256,2,1,256]{3,6,1,4,5,2,0:T(8,128)(2,1)} %copy.93) | copy-start | bytes 3145732
Sparse Core Ops, SparseCore 0:
  10.8 55.0 all-gather.10
  67.4 81.2 all-gather.8
  151.2 52.4 all-gather.14
  205.7 81.2 all-gather.12
  288.4 79.2 all-gather.16
  369.7 78.7 all-gather.18

commit v2 on v1

v2 whole, which is shorter than its diff:
```python
import functools

import jax
import jax.numpy as jnp
from jax import lax
from jax.experimental import pallas as pl
from jax.experimental.pallas import tpu as pltpu
from jax.sharding import PartitionSpec as P

OWN, NEAR = 0, 1
RIGHT, LEFT = 0, 1


def kernel(
    row_devices, col_devices, rows_loc, blk, cols_loc, diag_cols,
    s_in, u_in, d_in,
    o_all, d_out,
    u_buf, s_buf, o_mine, o_stage, acc,
    ring_send, ring_recv, sib_send, sib_recv, s_send, s_recv, near_send, near_recv,
    o_send, o_recv, mine_send, mine_recv, own_sem, keep_sem,
):
    nodes = s_in.shape[0]
    rows = rows_loc * blk
    chips = row_devices // 2
    half = chips // 2
    last = col_devices - 1
    p = lax.axis_index("prow")
    q = lax.axis_index("pcol")
    core = lax.rem(p, 2)
    flip = 1 - 2 * core
    inner = (q >= 1) & (q <= last - 1)
    helper = (q == 1) | (q == last - 1)
    end = (q == 0) | (q == last)
    near_q = jnp.where(q <= 1, 0, last)

    def along(n):
        high = n // half
        return n + high * (3 * half - 1 - 2 * n)

    chip = p // 2
    pos = along(chip)

    def slot(off):
        return along(lax.rem(pos + off + chips, chips)) * 2 + core

    def remote(src, dst, send, recv, to_p, to_q):
        return pltpu.make_async_remote_copy(
            src_ref=src, dst_ref=dst, send_sem=send, recv_sem=recv,
            device_id=(to_p, to_q), device_id_type=pl.DeviceIdType.MESH,
        )

    barrier = pltpu.get_barrier_semaphore()
    for step in range(1, row_devices):
        pl.semaphore_signal(
            barrier, inc=1, device_id=(lax.rem(p + step, row_devices), q),
            device_id_type=pl.DeviceIdType.MESH,
        )

    @pl.when(q > 0)
    def _():
        pl.semaphore_signal(
            barrier, inc=1, device_id=(p, q - 1), device_id_type=pl.DeviceIdType.MESH
        )

    @pl.when(q < last)
    def _():
        pl.semaphore_signal(
            barrier, inc=1, device_id=(p, q + 1), device_id_type=pl.DeviceIdType.MESH
        )

    @pl.when(inner)
    def _():
        pl.semaphore_wait(barrier, row_devices + 1)

    @pl.when(end)
    def _():
        pl.semaphore_wait(barrier, row_devices)

    def part(which, sn, at, step, way):
        if step < half:
            return u_buf.at[which, sn, at]
        cut = rows // 2
        return u_buf.at[which, sn, at, pl.ds(0 if way == RIGHT else cut, cut)]

    def ring(which, sn, way, step):
        sign = 1 if way == RIGHT else -1
        at = slot(-sign * (step - 1))
        dst = part(which, sn, at, step, way)
        src = u_in.at[sn] if (which == OWN and step == 1 and half > 1) else dst
        return remote(
            src, dst, ring_send.at[which, sn, way, step - 1],
            ring_recv.at[which, sn, way, step - 1], slot(sign), q,
        )

    def ring_wait(which, sn, way, step):
        sign = 1 if way == RIGHT else -1
        here = part(which, sn, slot(-sign * step), step, way)
        remote(
            here, here, ring_send.at[which, sn, way, step - 1],
            ring_recv.at[which, sn, way, step - 1], slot(sign), q,
        ).wait_recv()

    def sib(which, sn, off):
        at = slot(off)
        dst = u_buf.at[which, sn, at]
        src = u_in.at[sn] if (which == OWN and off == 0) else dst
        return remote(
            src, dst, sib_send.at[which, sn, off + half - 1],
            sib_recv.at[which, sn, off + half - 1], p + flip, q,
        )

    def sib_wait(which, sn, off):
        here = u_buf.at[which, sn, slot(off) + flip]
        remote(
            here, here, sib_send.at[which, sn, off + half - 1],
            sib_recv.at[which, sn, off + half - 1], p + flip, q,
        ).wait_recv()

    def ring_begin(which, sn):
        ring(which, sn, RIGHT, 1).start()
        ring(which, sn, LEFT, 1).start()
        sib(which, sn, 0).start()

    def ring_step(which, sn, step):
        for way in (RIGHT, LEFT):
            ring_wait(which, sn, way, step)
            if step < half:
                ring(which, sn, way, step + 1).start()
                sib(which, sn, -step if way == RIGHT else step).start()
        if step == half:
            sib(which, sn, half).start()

    def sib_all(which, sn):
        for off in range(1 - half, half + 1):
            sib_wait(which, sn, off)

    def ring_sent(which, sn):
        for step in range(1, half + 1):
            ring(which, sn, RIGHT, step).wait_send()
            ring(which, sn, LEFT, step).wait_send()
        for off in range(1 - half, half + 1):
            sib(which, sn, off).wait_send()

    def s_copy(sn, at, way):
        src = s_buf.at[sn, at]
        return remote(
            src, src, s_send.at[sn, at, way], s_recv.at[sn, at], p,
            q + 1 if way == RIGHT else q - 1,
        )

    def s_own(sn, way):
        return remote(
            s_in.at[sn], s_buf.at[sn, q], s_send.at[sn, q, way], s_recv.at[sn, q], p,
            q + 1 if way == RIGHT else q - 1,
        )

    up_ok = q + 1 <= last - 1
    down_ok = q - 1 >= 1

    def s_begin(sn):
        @pl.when(up_ok)
        def _():
            s_own(sn, RIGHT).start()

        @pl.when(down_ok)
        def _():
            s_own(sn, LEFT).start()

    def s_sent(sn):
        @pl.when(up_ok)
        def _():
            s_own(sn, RIGHT).wait_send()

        @pl.when(down_ok)
        def _():
            s_own(sn, LEFT).wait_send()

        for dist in range(1, col_devices):
            @pl.when((q - dist >= 0) & inner & up_ok)
            def _():
                s_copy(sn, q - dist, RIGHT).wait_send()

            @pl.when((q + dist <= last) & inner & down_ok)
            def _():
                s_copy(sn, q + dist, LEFT).wait_send()

    def s_step(sn, dist):
        for way, at, there, onward in (
            (RIGHT, q - dist, q - dist >= 0, up_ok),
            (LEFT, q + dist, q + dist <= last, down_ok),
        ):
            @pl.when(there & inner)
            def _():
                s_copy(sn, at, way).wait_recv()

                @pl.when(onward)
                def _():
                    s_copy(sn, at, way).start()

    def near(sn):
        return remote(
            u_in.at[sn], u_buf.at[NEAR, sn, p], near_send.at[sn], near_recv.at[sn], p,
            jnp.where(q == 0, 1, jnp.where(q == last, last - 1, near_q)),
        )

    def o_copy(sn, at, way, src=None):
        dst = o_all.at[sn, at]
        return remote(
            dst if src is None else src, dst, o_send.at[sn, at, way], o_recv.at[sn, at], p,
            q + 1 if way == RIGHT else q - 1,
        )

    def mine_each(sn, at, remote_do, local_do):
        for m in range(cols_loc):
            v = at + col_devices * m
            to_p = lax.rem(v, row_devices)
            k = v // row_devices
            if remote_do is not None:
                @pl.when(to_p != p)
                def _():
                    remote_do(
                        remote(
                            o_all.at[sn, at, m], o_mine.at[sn, k, p],
                            mine_send.at[sn, at, m], mine_recv.at[sn, k, p], to_p, q,
                        )
                    )

            if local_do is not None:
                @pl.when(to_p == p)
                def _():
                    local_do(
                        pltpu.make_async_copy(
                            o_all.at[sn, at, m], o_mine.at[sn, k, p], mine_recv.at[sn, k, p]
                        )
                    )

    def hand_out(sn, at):
        mine_each(sn, at, lambda c: c.start(), lambda c: c.start())

    def make_o(sn, which, at):
        for off in range(1 - half, half + 1):
            sib_wait(which, sn, off)
        acc[...] = jnp.zeros_like(acc)

        def add(src_p, carry):
            left = jnp.concatenate(
                [
                    s_buf[
                        sn, lax.rem(a * row_devices + src_p, col_devices),
                        (a * row_devices + src_p) // col_devices,
                    ]
                    for a in range(rows_loc)
                ],
                axis=1,
            )
            for m in range(cols_loc):
                acc[:rows, m * blk : (m + 1) * blk] += jnp.dot(
                    left, u_buf[which, sn, src_p, :, m * blk : (m + 1) * blk],
                    preferred_element_type=jnp.float32,
                )
            return carry

        lax.fori_loop(0, row_devices, add, 0)
        for m in range(cols_loc):
            o_stage[sn, which, m] = (-acc[:rows, m * blk : (m + 1) * blk]).astype(o_stage.dtype)
        stage = o_stage.at[sn, which]
        o_copy(sn, at, RIGHT, stage).start()
        o_copy(sn, at, LEFT, stage).start()
        keep = pltpu.make_async_copy(stage, o_all.at[sn, at], keep_sem.at[sn, which])
        keep.start()
        keep.wait()
        hand_out(sn, at)

    def o_step(sn, dist, extra):
        for way, origin, there, onward in (
            (RIGHT, q - dist, q - dist >= 1, q < last),
            (LEFT, q + dist, q + dist <= last - 1, q > 0),
        ):
            if extra:
                there = there & ((origin == 1) | (origin == last - 1))
                at = jnp.where(origin == 1, 0, last)
            else:
                at = origin
            @pl.when(there)
            def _():
                o_copy(sn, at, way).wait_recv()

                @pl.when(onward)
                def _():
                    o_copy(sn, at, way).start()

                hand_out(sn, at)

    def o_sent(sn):
        for extra in (False, True):
            if extra:
                first = helper
                at = near_q
            else:
                first = inner
                at = q
            @pl.when(first)
            def _():
                o_copy(sn, at, RIGHT).wait_send()
                o_copy(sn, at, LEFT).wait_send()
                mine_each(sn, at, lambda c: c.wait_send(), None)

            for dist in range(1, col_devices - 1):
                for way, origin, there, onward in (
                    (RIGHT, q - dist, q - dist >= 1, q < last),
                    (LEFT, q + dist, q + dist <= last - 1, q > 0),
                ):
                    if extra:
                        there = there & ((origin == 1) | (origin == last - 1))
                        at = jnp.where(origin == 1, 0, last)
                    else:
                        at = origin
                    @pl.when(there & onward)
                    def _():
                        o_copy(sn, at, way).wait_send()

                    @pl.when(there)
                    def _():
                        mine_each(sn, at, lambda c: c.wait_send(), None)

    def make_d(sn):
        acc[...] = jnp.zeros_like(acc)

        def add(src_p, carry):
            for k in range(diag_cols):
                pltpu.make_async_copy(
                    o_mine.at[sn, k, src_p], o_mine.at[sn, k, src_p], mine_recv.at[sn, k, src_p]
                ).wait()
                block = o_mine[sn, k, src_p]
                for m in range(cols_loc):
                    acc[k * blk : (k + 1) * blk, m * blk : (m + 1) * blk] += lax.dot_general(
                        block, u_buf[OWN, sn, src_p, :, m * blk : (m + 1) * blk],
                        (((0,), (0,)), ((), ())), preferred_element_type=jnp.float32,
                    )
            return carry

        lax.fori_loop(0, row_devices, add, 0)
        for k in range(diag_cols):
            for m in range(cols_loc):
                inner_sum = acc[k * blk : (k + 1) * blk, m * blk : (m + 1) * blk].T
                given = d_in[sn, m * blk : (m + 1) * blk, k * blk : (k + 1) * blk]
                d_out[sn, m * blk : (m + 1) * blk, k * blk : (k + 1) * blk] = (
                    given.astype(jnp.float32) - inner_sum
                ).astype(d_out.dtype)

    for sn in range(nodes):
        pltpu.make_async_copy(u_in.at[sn], u_buf.at[OWN, sn, p], own_sem.at[0, sn]).start()
        pltpu.make_async_copy(s_in.at[sn], s_buf.at[sn, q], own_sem.at[1, sn]).start()

    def near_begin(sn):
        @pl.when(end)
        def _():
            near(sn).start()

    s_begin(0)
    near_begin(0)
    ring_begin(OWN, 0)
    for sn in range(nodes):
        pltpu.make_async_copy(u_in.at[sn], u_buf.at[OWN, sn, p], own_sem.at[0, sn]).wait()
        pltpu.make_async_copy(s_in.at[sn], s_buf.at[sn, q], own_sem.at[1, sn]).wait()

    for sn in range(nodes):
        ring_step(OWN, sn, 1)
        s_step(sn, 1)
        if sn + 1 < nodes:
            s_begin(sn + 1)
            near_begin(sn + 1)
            ring_begin(OWN, sn + 1)

        @pl.when(helper)
        def _():
            near(sn).wait_recv()
            ring_begin(NEAR, sn)

        for step in range(2, half + 1):
            ring_step(OWN, sn, step)
        for dist in range(2, col_devices):
            s_step(sn, dist)

        if sn + 1 == nodes:
            @pl.when(helper)
            def _():
                for step in range(1, half + 1):
                    for other in range(nodes):
                        ring_step(NEAR, other, step)

        @pl.when(inner)
        def _():
            make_o(sn, OWN, q)

        @pl.when(end)
        def _():
            sib_all(OWN, sn)

    for sn in range(nodes):
        @pl.when(helper)
        def _():
            make_o(sn, NEAR, near_q)

        for dist in range(1, col_devices - 1):
            o_step(sn, dist, False)
        for dist in range(1, col_devices - 1):
            o_step(sn, dist, True)

    for sn in range(nodes):
        make_d(sn)

    for sn in range(nodes):
        ring_sent(OWN, sn)
        s_sent(sn)
        o_sent(sn)

        @pl.when(helper)
        def _():
            ring_sent(NEAR, sn)

        @pl.when(end)
        def _():
            near(sn).wait_send()


def on_device(anc_inverse, factor_panel, diag_inverse, block_pattern):
    row_index = lax.axis_index("prow")
    col_index = lax.axis_index("pcol")
    row_devices = lax.axis_size("prow")
    col_devices = lax.axis_size("pcol")
    nodes, rows_loc, _, blk, cols_loc, _, _ = anc_inverse.shape
    panel_cols = factor_panel.shape[4]
    diag_cols = diag_inverse.shape[4]
    rows = rows_loc * blk
    pattern_grid = block_pattern.reshape(nodes, rows_loc, row_devices, cols_loc, col_devices)
    owned = lax.dynamic_slice_in_dim(pattern_grid, row_index, 1, 2)
    owned = lax.dynamic_slice_in_dim(owned, col_index, 1, 4)
    masked = jnp.where(owned[:, :, :, None, :, :, None] != 0, anc_inverse, jnp.zeros_like(anc_inverse))
    s_in = masked.reshape(nodes, rows, cols_loc, blk).transpose(0, 2, 1, 3)
    u_in = factor_panel.reshape(nodes, rows, panel_cols * blk)
    d_in = diag_inverse.reshape(nodes, panel_cols * blk, diag_cols * blk)
    half = row_devices // 4
    dma = pltpu.SemaphoreType.DMA
    bf16 = jnp.bfloat16
    o_all, d_out = pl.pallas_call(
        functools.partial(
            kernel, row_devices, col_devices, rows_loc, blk, panel_cols, diag_cols
        ),
        out_shape=(
            jax.ShapeDtypeStruct((nodes, col_devices, panel_cols, rows, blk), bf16),
            jax.ShapeDtypeStruct(d_in.shape, bf16),
        ),
        in_specs=[
            pl.BlockSpec(memory_space=pl.ANY),
            pl.BlockSpec(memory_space=pl.ANY),
            pl.BlockSpec(memory_space=pltpu.VMEM),
        ],
        out_specs=(
            pl.BlockSpec(memory_space=pl.ANY),
            pl.BlockSpec(memory_space=pltpu.VMEM),
        ),
        scratch_shapes=[
            pltpu.VMEM((2, nodes, row_devices, rows, panel_cols * blk), bf16),
            pltpu.VMEM((nodes, col_devices, cols_loc, rows, blk), bf16),
            pltpu.VMEM((nodes, diag_cols, row_devices, rows, blk), bf16),
            pltpu.VMEM((nodes, 2, panel_cols, rows, blk), bf16),
            pltpu.VMEM((max(rows, diag_cols * blk), panel_cols * blk), jnp.float32),
            dma((2, nodes, 2, half)),
            dma((2, nodes, 2, half)),
            dma((2, nodes, 2 * half)),
            dma((2, nodes, 2 * half)),
            dma((nodes, col_devices, 2)),
            dma((nodes, col_devices)),
            dma((nodes,)),
            dma((nodes,)),
            dma((nodes, col_devices, 2)),
            dma((nodes, col_devices)),
            dma((nodes, col_devices, panel_cols)),
            dma((nodes, diag_cols, row_devices)),
            dma((2, nodes)),
            dma((nodes, 2)),
        ],
        compiler_params=pltpu.CompilerParams(
            collective_id=0, has_side_effects=True, vmem_limit_bytes=62 * 1024 * 1024
        ),
        cost_estimate=pl.CostEstimate(
            flops=18 * 10**9, bytes_accessed=40 * 2**20, transcendentals=0
        ),
    )(s_in, u_in, d_in)
    off = lax.dynamic_slice_in_dim(o_all, col_index, 1, 1)[:, 0]
    sigma_off = off.transpose(0, 2, 1, 3).reshape(factor_panel.shape)
    return (sigma_off, d_out.reshape(diag_inverse.shape))


def solution(mesh):
    return jax.shard_map(
        on_device,
        mesh=mesh,
        in_specs=(
            P(None, None, "prow", None, None, "pcol", None),
            P(None, None, "prow", None, None, "pcol", None),
            P(None, None, "pcol", None, None, "prow", None),
            P(),
        ),
        out_specs=(
            P(None, None, "prow", None, None, "pcol", None),
            P(None, None, "pcol", None, None, "prow", None),
        ),
        check_vma=False,
    )
```

time: 535 us -> 383 us (0.72)
  waiting for transfers between devices: 404 us -> 0 us
  Pallas kernels: 0 us -> 363 us
  local copies, waits for them, and re-layouts: 60.5 us -> 17.1 us
  matrix products: 38.6 us -> 0 us
  between operations: 14.2 us -> 0.68 us
  starting transfers between devices: 10.6 us -> 0 us
    all_gather x6 -> x0, waiting for transfers between devices: 379 us -> none  [the longest x2 151 us: invert_window(): masked_all = lax.all_gather(masked, 'pcol', axis=5, tiled=True)]
    pallas_call x0 -> x1, Pallas kernels: none -> 363 us  [on_device(): pl.pallas_call(functools.partial(kernel, row_devices, col_devices, rows_l...]
    dot_general x4 -> x0, matrix products: 38.6 us -> none  [the longest x2 20.3 us: invert_window(): jnp.einsum('sraicbj,scbjwm->sraiwm', masked_all, panel_rows, preferred_el...]
    all_gather x4 -> x0, local copies, waits for them, and re-layouts: 27.7 us -> none  [the longest x2 15.3 us: invert_window(): panel_all = lax.all_gather(panel_local, 'prow', axis=2, tiled=True)]
    all_to_all x2 -> x0, waiting for transfers between devices: 24.8 us -> none  [invert_window(): lax.all_to_all(by_owner, 'prow', split_axis=5, concat_axis=2, tiled=True)]
    unnamed x19 -> x7, local copies, waits for them, and re-layouts: 14.9 us -> 4.43 us
    all_to_all x2 -> x0, starting transfers between devices: 10.3 us -> none  [invert_window(): lax.all_to_all(by_owner, 'prow', split_axis=5, concat_axis=2, tiled=True)]
    slice x3 -> x0, local copies, waits for them, and re-layouts: 8.13 us -> none  [the longest x1 3.6 us: on_device(): diag_inverse[supernode:supernode + 1]]
  transfers between devices with their start and end apart: 8 -> 0, of which waited for: 7 -> 0; matrix products, arithmetic and copies ran while one was open for 16% -> 0% of each run, Pallas kernels for 0% -> 0%
where the time goes in v2:
time: 383 us
  Pallas kernels  363 us (95%)
  local copies, waits for them, and re-layouts  17.1 us (4%)
    pallas_call x1, Pallas kernels, on_device(): pl.pallas_call(functools.partial(kernel, row_devices, col_devices, rows_l...  363 us

profile of v2, /device:TPU:7, one launch (start us, length us, event | category | flops | bytes accessed | tf_op | source)
XLA Modules:
  0.0 383.0 jit_solution(15122015352890786546)
XLA Ops:
  0.6 0.8 copy.14
  1.4 0.1 reshape.33
  1.5 0.1 constant_dynamic-slice_fusion.1
  1.6 0.1 copy.19
  1.7 2.5 broadcast_select_fusion
  4.2 0.0 copy-start
  4.2 1.7 copy.16
  5.9 0.6 copy-done
  6.5 2.7 reshape.35.u_in
  9.2 4.4 %reshape.36.d_in = bf16[2,1024,512]{2,1,0:T(8,128)(2,1)} reshape(bf16[2,4,1,256,2,1,256]{6,4,5,3,2,1,0:T(2,128)(2,1)} %param.6) | data formatting | bytes 4194304 | tf_op jit(solution)/shard_map/reshape | solution.py:442
  13.6 362.7 %shard_map.59 = (bf16[2,4,4,512,256]{4,3,2,1,0:T(8,128)(2,1)}, bf16[2,1024,512]{2,1,0:T(8,128)(2,1)}) custom-call(bf16[2,4,512,256]{3,2,1,0:T(8,128)(2,1)} %bitcast.19, bf16[2,512,1024]{2,1,0:T(8,128)(2,1)} %reshape.35.u_in, bf16[2,1024,512]{2,1,0:T(8,128)(2,1)} %reshape.36.d_in), custom_call_target="tpu_custom_call" | custom-call | flops 17999998976 | bytes 41943040 | tf_op jit(solution)/shard_map/pallas_call | solution.py:446
  376.3 1.7 constant_dynamic-slice_fusion
  378.1 0.0 copy-start.1
  378.1 2.9 copy.17
  381.0 0.0 copy-done.1
  381.0 2.0 reshape.38
  (1 shorter events, 0.0 us)
Async XLA Ops:
  4.2 2.3 copy-start
  378.1 3.0 copy-start.1

commit v3 on v2

--- a/solution.py
+++ b/solution.py
@@ -104,16 +104,19 @@
         at = slot(off)
         dst = u_buf.at[which, sn, at]
         src = u_in.at[sn] if (which == OWN and off == 0) else dst
-        return remote(
-            src, dst, sib_send.at[which, sn, off + half - 1],
-            sib_recv.at[which, sn, off + half - 1], p + flip, q,
-        )
+        index = off + half - (which == OWN)
+        return remote(
+            src, dst, sib_send.at[which, sn, index], sib_recv.at[which, sn, index], p + flip, q
+        )
+
+    def offsets(which):
+        return range(1 - half, half + 1) if which == OWN else range(-half, half)
 
     def sib_wait(which, sn, off):
         here = u_buf.at[which, sn, slot(off) + flip]
+        index = off + half - (which == OWN)
         remote(
-            here, here, sib_send.at[which, sn, off + half - 1],
-            sib_recv.at[which, sn, off + half - 1], p + flip, q,
+            here, here, sib_send.at[which, sn, index], sib_recv.at[which, sn, index], p + flip, q
         ).wait_recv()
 
     def ring_begin(which, sn):
@@ -131,15 +134,43 @@
             sib(which, sn, half).start()
 
     def sib_all(which, sn):
-        for off in range(1 - half, half + 1):
+        for off in offsets(which):
             sib_wait(which, sn, off)
 
     def ring_sent(which, sn):
-        for step in range(1, half + 1):
-            ring(which, sn, RIGHT, step).wait_send()
-            ring(which, sn, LEFT, step).wait_send()
-        for off in range(1 - half, half + 1):
+        for step in range(1, half + (which == OWN)):
+            for way in (RIGHT, LEFT):
+                (ring if which == OWN else near_ring)(which, sn, way, step).wait_send()
+        for off in offsets(which):
             sib(which, sn, off).wait_send()
+
+    def near_ring(which, sn, way, step):
+        at = slot(-step if way == RIGHT else step - 1)
+        src = u_buf.at[which, sn, at]
+        return remote(
+            src, src, ring_send.at[which, sn, way, step - 1],
+            ring_recv.at[which, sn, way, step - 1], slot(1 if way == RIGHT else -1), q,
+        )
+
+    def near_arrived(sn):
+        for index in (0, 1):
+            near(sn, index).wait_recv()
+            if half > 1:
+                near_ring(NEAR, sn, LEFT if index == 0 else RIGHT, 1).start()
+            sib(NEAR, sn, -index).start()
+
+    def near_steps(sn):
+        for step in range(1, half):
+            for way in (RIGHT, LEFT):
+                off = -step - 1 if way == RIGHT else step
+                here = u_buf.at[NEAR, sn, slot(off)]
+                remote(
+                    here, here, ring_send.at[NEAR, sn, way, step - 1],
+                    ring_recv.at[NEAR, sn, way, step - 1], slot(1 if way == RIGHT else -1), q,
+                ).wait_recv()
+                if step + 1 < half:
+                    near_ring(NEAR, sn, way, step + 1).start()
+                sib(NEAR, sn, off).start()
 
     def s_copy(sn, at, way):
         src = s_buf.at[sn, at]
@@ -197,9 +228,11 @@
                 def _():
                     s_copy(sn, at, way).start()
 
-    def near(sn):
-        return remote(
-            u_in.at[sn], u_buf.at[NEAR, sn, p], near_send.at[sn], near_recv.at[sn], p,
+    def near(sn, index):
+        src = u_in.at[sn] if index == 0 else u_buf.at[OWN, sn, slot(-1)]
+        return remote(
+            src, u_buf.at[NEAR, sn, slot(-index)], near_send.at[sn, index],
+            near_recv.at[sn, index], p,
             jnp.where(q == 0, 1, jnp.where(q == last, last - 1, near_q)),
         )
 
@@ -238,8 +271,7 @@
         mine_each(sn, at, lambda c: c.start(), lambda c: c.start())
 
     def make_o(sn, which, at):
-        for off in range(1 - half, half + 1):
-            sib_wait(which, sn, off)
+        sib_all(which, sn)
         acc[...] = jnp.zeros_like(acc)
 
         def add(src_p, carry):
@@ -352,13 +384,26 @@
         pltpu.make_async_copy(u_in.at[sn], u_buf.at[OWN, sn, p], own_sem.at[0, sn]).start()
         pltpu.make_async_copy(s_in.at[sn], s_buf.at[sn, q], own_sem.at[1, sn]).start()
 
-    def near_begin(sn):
+    def near_begin(sn, index):
         @pl.when(end)
         def _():
-            near(sn).start()
+            near(sn, index).start()
+
+    def main_o(sn):
+        @pl.when(inner)
+        def _():
+            make_o(sn, OWN, q)
+
+        @pl.when(end)
+        def _():
+            sib_all(OWN, sn)
+
+    def o_steps(sn, extra):
+        for dist in range(1, col_devices - 1):
+            o_step(sn, dist, extra)
 
     s_begin(0)
-    near_begin(0)
+    near_begin(0, 0)
     ring_begin(OWN, 0)
     for sn in range(nodes):
         pltpu.make_async_copy(u_in.at[sn], u_buf.at[OWN, sn, p], own_sem.at[0, sn]).wait()
@@ -366,46 +411,37 @@
 
     for sn in range(nodes):
         ring_step(OWN, sn, 1)
-        s_step(sn, 1)
+        near_begin(sn, 1)
         if sn + 1 < nodes:
             s_begin(sn + 1)
-            near_begin(sn + 1)
+            near_begin(sn + 1, 0)
             ring_begin(OWN, sn + 1)
-
-        @pl.when(helper)
-        def _():
-            near(sn).wait_recv()
-            ring_begin(NEAR, sn)
-
+        if sn > 0:
+            @pl.when(helper)
+            def _():
+                near_arrived(sn - 1)
+
+        s_step(sn, 1)
         for step in range(2, half + 1):
             ring_step(OWN, sn, step)
         for dist in range(2, col_devices):
             s_step(sn, dist)
-
-        if sn + 1 == nodes:
-            @pl.when(helper)
-            def _():
-                for step in range(1, half + 1):
-                    for other in range(nodes):
-                        ring_step(NEAR, other, step)
-
-        @pl.when(inner)
-        def _():
-            make_o(sn, OWN, q)
-
-        @pl.when(end)
-        def _():
-            sib_all(OWN, sn)
-
-    for sn in range(nodes):
+        main_o(sn)
+
+    @pl.when(helper)
+    def _():
+        near_arrived(nodes - 1)
+
+    for sn in range(nodes):
+        o_steps(sn, False)
+
         @pl.when(helper)
         def _():
+            near_steps(sn)
             make_o(sn, NEAR, near_q)
 
-        for dist in range(1, col_devices - 1):
-            o_step(sn, dist, False)
-        for dist in range(1, col_devices - 1):
-            o_step(sn, dist, True)
+    for sn in range(nodes):
+        o_steps(sn, True)
 
     for sn in range(nodes):
         make_d(sn)
@@ -421,7 +457,8 @@
 
         @pl.when(end)
         def _():
-            near(sn).wait_send()
+            near(sn, 0).wait_send()
+            near(sn, 1).wait_send()
 
 
 def on_device(anc_inverse, factor_panel, diag_inverse, block_pattern):
@@ -472,8 +509,8 @@
             dma((2, nodes, 2 * half)),
             dma((nodes, col_devices, 2)),
             dma((nodes, col_devices)),
-            dma((nodes,)),
-            dma((nodes,)),
+            dma((nodes, 2)),
+            dma((nodes, 2)),
             dma((nodes, col_devices, 2)),
             dma((nodes, col_devices)),
             dma((nodes, col_devices, panel_cols)),

time: 383 us -> 344 us (0.90)
  Pallas kernels: 363 us -> 324 us
    pallas_call x1, Pallas kernels: 363 us -> 324 us  [on_device(): pl.pallas_call(functools.partial(kernel, row_devices, col_devices, rows_l...]
where the time goes in v3:
time: 344 us
  Pallas kernels  324 us (94%)
  local copies, waits for them, and re-layouts  17.1 us (5%)
    pallas_call x1, Pallas kernels, on_device(): pl.pallas_call(functools.partial(kernel, row_devices, col_devices, rows_l...  324 us

profile of v3, /device:TPU:7, one launch (start us, length us, event | category | flops | bytes accessed | tf_op | source)
XLA Modules:
  0.0 344.1 jit_solution(16498825644277397519)
XLA Ops:
  0.6 0.8 copy.14
  1.4 0.1 reshape.33
  1.5 0.1 constant_dynamic-slice_fusion.1
  1.6 0.1 copy.19
  1.7 2.5 broadcast_select_fusion
  4.2 0.0 copy-start
  4.2 1.7 copy.16
  5.9 0.6 copy-done
  6.5 2.7 reshape.35.u_in
  9.2 4.4 %reshape.36.d_in = bf16[2,1024,512]{2,1,0:T(8,128)(2,1)} reshape(bf16[2,4,1,256,2,1,256]{6,4,5,3,2,1,0:T(2,128)(2,1)} %param.6) | data formatting | bytes 4194304 | tf_op jit(solution)/shard_map/reshape | solution.py:479
  13.6 323.8 %shard_map.59 = (bf16[2,4,4,512,256]{4,3,2,1,0:T(8,128)(2,1)}, bf16[2,1024,512]{2,1,0:T(8,128)(2,1)}) custom-call(bf16[2,4,512,256]{3,2,1,0:T(8,128)(2,1)} %bitcast.19, bf16[2,512,1024]{2,1,0:T(8,128)(2,1)} %reshape.35.u_in, bf16[2,1024,512]{2,1,0:T(8,128)(2,1)} %reshape.36.d_in), custom_call_target="tpu_custom_call" | custom-call | flops 17999998976 | bytes 41943040 | tf_op jit(solution)/shard_map/pallas_call | solution.py:483
  337.4 1.7 constant_dynamic-slice_fusion
  339.1 0.0 copy-start.1
  339.1 2.9 copy.17
  342.1 0.0 copy-done.1
  342.1 2.0 reshape.38
  (1 shorter events, 0.0 us)
Async XLA Ops:
  4.2 2.3 copy-start
  339.1 3.0 copy-start.1

commit v4 on v3

--- a/solution.py
+++ b/solution.py
@@ -22,6 +22,7 @@
     nodes = s_in.shape[0]
     rows = rows_loc * blk
     chips = row_devices // 2
+    group = 4 if row_devices % 4 == 0 else 1
     half = chips // 2
     last = col_devices - 1
     p = lax.axis_index("prow")
@@ -40,6 +41,9 @@
     chip = p // 2
     pos = along(chip)
 
+    def panel(which, sn):
+        return sn if which == OWN else nodes
+
     def slot(off):
         return along(lax.rem(pos + off + chips, chips)) * 2 + core
 
@@ -78,9 +82,9 @@
 
     def part(which, sn, at, step, way):
         if step < half:
-            return u_buf.at[which, sn, at]
+            return u_buf.at[panel(which, sn), at]
         cut = rows // 2
-        return u_buf.at[which, sn, at, pl.ds(0 if way == RIGHT else cut, cut)]
+        return u_buf.at[panel(which, sn), at, pl.ds(0 if way == RIGHT else cut, cut)]
 
     def ring(which, sn, way, step):
         sign = 1 if way == RIGHT else -1
@@ -102,7 +106,7 @@
 
     def sib(which, sn, off):
         at = slot(off)
-        dst = u_buf.at[which, sn, at]
+        dst = u_buf.at[panel(which, sn), at]
         src = u_in.at[sn] if (which == OWN and off == 0) else dst
         index = off + half - (which == OWN)
         return remote(
@@ -113,7 +117,7 @@
         return range(1 - half, half + 1) if which == OWN else range(-half, half)
 
     def sib_wait(which, sn, off):
-        here = u_buf.at[which, sn, slot(off) + flip]
+        here = u_buf.at[panel(which, sn), slot(off) + flip]
         index = off + half - (which == OWN)
         remote(
             here, here, sib_send.at[which, sn, index], sib_recv.at[which, sn, index], p + flip, q
@@ -146,7 +150,7 @@
 
     def near_ring(which, sn, way, step):
         at = slot(-step if way == RIGHT else step - 1)
-        src = u_buf.at[which, sn, at]
+        src = u_buf.at[panel(which, sn), at]
         return remote(
             src, src, ring_send.at[which, sn, way, step - 1],
             ring_recv.at[which, sn, way, step - 1], slot(1 if way == RIGHT else -1), q,
@@ -163,7 +167,7 @@
         for step in range(1, half):
             for way in (RIGHT, LEFT):
                 off = -step - 1 if way == RIGHT else step
-                here = u_buf.at[NEAR, sn, slot(off)]
+                here = u_buf.at[panel(NEAR, sn), slot(off)]
                 remote(
                     here, here, ring_send.at[NEAR, sn, way, step - 1],
                     ring_recv.at[NEAR, sn, way, step - 1], slot(1 if way == RIGHT else -1), q,
@@ -185,42 +189,54 @@
             q + 1 if way == RIGHT else q - 1,
         )
 
-    up_ok = q + 1 <= last - 1
-    down_ok = q - 1 >= 1
+    def lent(sn):
+        return sn == 0
+
+    def span(sn):
+        return (1, last - 1) if lent(sn) else (0, last)
+
+    def s_up(sn):
+        return q + 1 <= span(sn)[1]
+
+    def s_down(sn):
+        return q - 1 >= span(sn)[0]
+
+    def s_here(sn):
+        return (q >= span(sn)[0]) & (q <= span(sn)[1])
 
     def s_begin(sn):
-        @pl.when(up_ok)
+        @pl.when(s_up(sn))
         def _():
             s_own(sn, RIGHT).start()
 
-        @pl.when(down_ok)
+        @pl.when(s_down(sn))
         def _():
             s_own(sn, LEFT).start()
 
     def s_sent(sn):
-        @pl.when(up_ok)
+        @pl.when(s_up(sn))
         def _():
             s_own(sn, RIGHT).wait_send()
 
-        @pl.when(down_ok)
+        @pl.when(s_down(sn))
         def _():
             s_own(sn, LEFT).wait_send()
 
         for dist in range(1, col_devices):
-            @pl.when((q - dist >= 0) & inner & up_ok)
+            @pl.when((q - dist >= 0) & s_here(sn) & s_up(sn))
             def _():
                 s_copy(sn, q - dist, RIGHT).wait_send()
 
-            @pl.when((q + dist <= last) & inner & down_ok)
+            @pl.when((q + dist <= last) & s_here(sn) & s_down(sn))
             def _():
                 s_copy(sn, q + dist, LEFT).wait_send()
 
     def s_step(sn, dist):
         for way, at, there, onward in (
-            (RIGHT, q - dist, q - dist >= 0, up_ok),
-            (LEFT, q + dist, q + dist <= last, down_ok),
+            (RIGHT, q - dist, q - dist >= 0, s_up(sn)),
+            (LEFT, q + dist, q + dist <= last, s_down(sn)),
         ):
-            @pl.when(there & inner)
+            @pl.when(there & s_here(sn))
             def _():
                 s_copy(sn, at, way).wait_recv()
 
@@ -229,9 +245,9 @@
                     s_copy(sn, at, way).start()
 
     def near(sn, index):
-        src = u_in.at[sn] if index == 0 else u_buf.at[OWN, sn, slot(-1)]
-        return remote(
-            src, u_buf.at[NEAR, sn, slot(-index)], near_send.at[sn, index],
+        src = u_in.at[sn] if index == 0 else u_buf.at[panel(OWN, sn), slot(-1)]
+        return remote(
+            src, u_buf.at[panel(NEAR, sn), slot(-index)], near_send.at[sn, index],
             near_recv.at[sn, index], p,
             jnp.where(q == 0, 1, jnp.where(q == last, last - 1, near_q)),
         )
@@ -274,30 +290,40 @@
         sib_all(which, sn)
         acc[...] = jnp.zeros_like(acc)
 
-        def add(src_p, carry):
+        def add(step, carry):
+            first = step * group
             left = jnp.concatenate(
                 [
                     s_buf[
-                        sn, lax.rem(a * row_devices + src_p, col_devices),
-                        (a * row_devices + src_p) // col_devices,
+                        sn, lax.rem(a * row_devices + first + i, col_devices),
+                        (a * row_devices + first + i) // col_devices,
                     ]
+                    for i in range(group)
                     for a in range(rows_loc)
                 ],
                 axis=1,
             )
             for m in range(cols_loc):
+                right = u_buf[
+                    panel(which, sn), pl.ds(first, group), :, m * blk : (m + 1) * blk
+                ].reshape(group * rows, blk)
                 acc[:rows, m * blk : (m + 1) * blk] += jnp.dot(
-                    left, u_buf[which, sn, src_p, :, m * blk : (m + 1) * blk],
-                    preferred_element_type=jnp.float32,
+                    left, right, preferred_element_type=jnp.float32
                 )
             return carry
 
-        lax.fori_loop(0, row_devices, add, 0)
+        lax.fori_loop(0, row_devices // group, add, 0)
         for m in range(cols_loc):
             o_stage[sn, which, m] = (-acc[:rows, m * blk : (m + 1) * blk]).astype(o_stage.dtype)
         stage = o_stage.at[sn, which]
-        o_copy(sn, at, RIGHT, stage).start()
-        o_copy(sn, at, LEFT, stage).start()
+        @pl.when(q < last)
+        def _():
+            o_copy(sn, at, RIGHT, stage).start()
+
+        @pl.when(q > 0)
+        def _():
+            o_copy(sn, at, LEFT, stage).start()
+
         keep = pltpu.make_async_copy(stage, o_all.at[sn, at], keep_sem.at[sn, which])
         keep.start()
         keep.wait()
@@ -305,8 +331,8 @@
 
     def o_step(sn, dist, extra):
         for way, origin, there, onward in (
-            (RIGHT, q - dist, q - dist >= 1, q < last),
-            (LEFT, q + dist, q + dist <= last - 1, q > 0),
+            (RIGHT, q - dist, q - dist >= span(sn)[0], q < last),
+            (LEFT, q + dist, q + dist <= span(sn)[1], q > 0),
         ):
             if extra:
                 there = there & ((origin == 1) | (origin == last - 1))
@@ -324,23 +350,30 @@
                 hand_out(sn, at)
 
     def o_sent(sn):
-        for extra in (False, True):
+        for extra in (False, True) if lent(sn) else (False,):
             if extra:
                 first = helper
                 at = near_q
             else:
-                first = inner
+                first = s_here(sn)
                 at = q
+
+            @pl.when(first & (q < last))
+            def _():
+                o_copy(sn, at, RIGHT).wait_send()
+
+            @pl.when(first & (q > 0))
+            def _():
+                o_copy(sn, at, LEFT).wait_send()
+
             @pl.when(first)
             def _():
-                o_copy(sn, at, RIGHT).wait_send()
-                o_copy(sn, at, LEFT).wait_send()
                 mine_each(sn, at, lambda c: c.wait_send(), None)
 
-            for dist in range(1, col_devices - 1):
+            for dist in range(1, span(sn)[1] + 1):
                 for way, origin, there, onward in (
-                    (RIGHT, q - dist, q - dist >= 1, q < last),
-                    (LEFT, q + dist, q + dist <= last - 1, q > 0),
+                    (RIGHT, q - dist, q - dist >= span(sn)[0], q < last),
+                    (LEFT, q + dist, q + dist <= span(sn)[1], q > 0),
                 ):
                     if extra:
                         there = there & ((origin == 1) | (origin == last - 1))
@@ -358,20 +391,24 @@
     def make_d(sn):
         acc[...] = jnp.zeros_like(acc)
 
-        def add(src_p, carry):
+        def add(step, carry):
+            first = step * group
             for k in range(diag_cols):
-                pltpu.make_async_copy(
-                    o_mine.at[sn, k, src_p], o_mine.at[sn, k, src_p], mine_recv.at[sn, k, src_p]
-                ).wait()
-                block = o_mine[sn, k, src_p]
+                for i in range(group):
+                    here = o_mine.at[sn, k, first + i]
+                    pltpu.make_async_copy(here, here, mine_recv.at[sn, k, first + i]).wait()
+                block = o_mine[sn, k, pl.ds(first, group)].reshape(group * rows, blk)
                 for m in range(cols_loc):
+                    right = u_buf[
+                        panel(OWN, sn), pl.ds(first, group), :, m * blk : (m + 1) * blk
+                    ].reshape(group * rows, blk)
                     acc[k * blk : (k + 1) * blk, m * blk : (m + 1) * blk] += lax.dot_general(
-                        block, u_buf[OWN, sn, src_p, :, m * blk : (m + 1) * blk],
-                        (((0,), (0,)), ((), ())), preferred_element_type=jnp.float32,
+                        block, right, (((0,), (0,)), ((), ())),
+                        preferred_element_type=jnp.float32,
                     )
             return carry
 
-        lax.fori_loop(0, row_devices, add, 0)
+        lax.fori_loop(0, row_devices // group, add, 0)
         for k in range(diag_cols):
             for m in range(cols_loc):
                 inner_sum = acc[k * blk : (k + 1) * blk, m * blk : (m + 1) * blk].T
@@ -381,67 +418,67 @@
                 ).astype(d_out.dtype)
 
     for sn in range(nodes):
-        pltpu.make_async_copy(u_in.at[sn], u_buf.at[OWN, sn, p], own_sem.at[0, sn]).start()
+        pltpu.make_async_copy(u_in.at[sn], u_buf.at[panel(OWN, sn), p], own_sem.at[0, sn]).start()
         pltpu.make_async_copy(s_in.at[sn], s_buf.at[sn, q], own_sem.at[1, sn]).start()
 
     def near_begin(sn, index):
-        @pl.when(end)
-        def _():
-            near(sn, index).start()
+        if lent(sn):
+            @pl.when(end)
+            def _():
+                near(sn, index).start()
 
     def main_o(sn):
-        @pl.when(inner)
+        @pl.when(s_here(sn))
         def _():
             make_o(sn, OWN, q)
 
-        @pl.when(end)
+        @pl.when(jnp.logical_not(s_here(sn)))
         def _():
             sib_all(OWN, sn)
 
-    def o_steps(sn, extra):
-        for dist in range(1, col_devices - 1):
-            o_step(sn, dist, extra)
-
-    s_begin(0)
-    near_begin(0, 0)
+    def lent_o(sn):
+        if lent(sn):
+            @pl.when(helper)
+            def _():
+                near_steps(sn)
+                make_o(sn, NEAR, near_q)
+
+    for sn in range(nodes):
+        near_begin(sn, 0)
+        s_begin(sn)
     ring_begin(OWN, 0)
     for sn in range(nodes):
-        pltpu.make_async_copy(u_in.at[sn], u_buf.at[OWN, sn, p], own_sem.at[0, sn]).wait()
+        pltpu.make_async_copy(u_in.at[sn], u_buf.at[panel(OWN, sn), p], own_sem.at[0, sn]).wait()
         pltpu.make_async_copy(s_in.at[sn], s_buf.at[sn, q], own_sem.at[1, sn]).wait()
 
     for sn in range(nodes):
         ring_step(OWN, sn, 1)
         near_begin(sn, 1)
         if sn + 1 < nodes:
-            s_begin(sn + 1)
-            near_begin(sn + 1, 0)
             ring_begin(OWN, sn + 1)
-        if sn > 0:
-            @pl.when(helper)
-            def _():
-                near_arrived(sn - 1)
-
-        s_step(sn, 1)
+        if sn == 0:
+            for other in range(nodes):
+                s_step(other, 1)
         for step in range(2, half + 1):
             ring_step(OWN, sn, step)
-        for dist in range(2, col_devices):
-            s_step(sn, dist)
+        if sn == 0:
+            for dist in range(2, col_devices - 1):
+                for other in range(nodes):
+                    s_step(other, dist)
+        s_step(sn, col_devices - 1)
         main_o(sn)
-
-    @pl.when(helper)
-    def _():
-        near_arrived(nodes - 1)
-
-    for sn in range(nodes):
-        o_steps(sn, False)
-
-        @pl.when(helper)
-        def _():
-            near_steps(sn)
-            make_o(sn, NEAR, near_q)
-
-    for sn in range(nodes):
-        o_steps(sn, True)
+        if lent(sn):
+            @pl.when(helper)
+            def _():
+                near_arrived(sn)
+
+    for dist in range(1, col_devices):
+        o_step(0, dist, False)
+    lent_o(0)
+    for dist in range(1, col_devices):
+        for sn in range(1, nodes):
+            o_step(sn, dist, False)
+        o_step(0, dist, True)
 
     for sn in range(nodes):
         make_d(sn)
@@ -451,14 +488,15 @@
         s_sent(sn)
         o_sent(sn)
 
-        @pl.when(helper)
-        def _():
-            ring_sent(NEAR, sn)
-
-        @pl.when(end)
-        def _():
-            near(sn, 0).wait_send()
-            near(sn, 1).wait_send()
+        if lent(sn):
+            @pl.when(helper)
+            def _():
+                ring_sent(NEAR, sn)
+
+            @pl.when(end)
+            def _():
+                near(sn, 0).wait_send()
+                near(sn, 1).wait_send()
 
 
 def on_device(anc_inverse, factor_panel, diag_inverse, block_pattern):
@@ -498,7 +536,7 @@
             pl.BlockSpec(memory_space=pltpu.VMEM),
         ),
         scratch_shapes=[
-            pltpu.VMEM((2, nodes, row_devices, rows, panel_cols * blk), bf16),
+            pltpu.VMEM((nodes + 1, row_devices, rows, panel_cols * blk), bf16),
             pltpu.VMEM((nodes, col_devices, cols_loc, rows, blk), bf16),
             pltpu.VMEM((nodes, diag_cols, row_devices, rows, blk), bf16),
             pltpu.VMEM((nodes, 2, panel_cols, rows, blk), bf16),

time: 344 us -> 361 us (1.049)
  Pallas kernels: 324 us -> 340 us
    pallas_call x1, Pallas kernels: 324 us -> 340 us  [on_device(): pl.pallas_call(functools.partial(kernel, row_devices, col_devices, rows_l...]
where the time goes in v4:
time: 361 us
  Pallas kernels  340 us (94%)
  local copies, waits for them, and re-layouts  17.1 us (5%)
    pallas_call x1, Pallas kernels, on_device(): pl.pallas_call(functools.partial(kernel, row_devices, col_devices, rows_l...  340 us

profile of v4, /device:TPU:7, one launch (start us, length us, event | category | flops | bytes accessed | tf_op | source)
XLA Modules:
  0.0 360.7 jit_solution(4499547266678135273)
XLA Ops:
  0.6 0.8 copy.14
  1.4 0.1 reshape.33
  1.5 0.1 constant_dynamic-slice_fusion.1
  1.6 0.1 copy.19
  1.7 2.5 broadcast_select_fusion
  4.2 0.0 copy-start
  4.2 1.7 copy.16
  5.9 0.6 copy-done
  6.5 2.7 reshape.35.u_in
  9.2 4.4 %reshape.36.d_in = bf16[2,1024,512]{2,1,0:T(8,128)(2,1)} reshape(bf16[2,4,1,256,2,1,256]{6,4,5,3,2,1,0:T(2,128)(2,1)} %param.6) | data formatting | bytes 4194304 | tf_op jit(solution)/shard_map/reshape | solution.py:517
  13.6 340.4 %shard_map.59 = (bf16[2,4,4,512,256]{4,3,2,1,0:T(8,128)(2,1)}, bf16[2,1024,512]{2,1,0:T(8,128)(2,1)}) custom-call(bf16[2,4,512,256]{3,2,1,0:T(8,128)(2,1)} %bitcast.19, bf16[2,512,1024]{2,1,0:T(8,128)(2,1)} %reshape.35.u_in, bf16[2,1024,512]{2,1,0:T(8,128)(2,1)} %reshape.36.d_in), custom_call_target="tpu_custom_call" | custom-call | flops 17999998976 | bytes 41943040 | tf_op jit(solution)/shard_map/pallas_call | solution.py:521
  354.0 1.7 constant_dynamic-slice_fusion
  355.7 0.0 copy-start.1
  355.7 2.9 copy.17
  358.6 0.0 copy-done.1
  358.6 2.0 reshape.38
  (1 shorter events, 0.0 us)
Async XLA Ops:
  4.2 2.3 copy-start
  355.7 3.0 copy-start.1

commit v5 on v4

--- a/solution.py
+++ b/solution.py
@@ -22,6 +22,8 @@
     nodes = s_in.shape[0]
     rows = rows_loc * blk
     chips = row_devices // 2
+    parts = 2 if cols_loc % 2 == 0 else 1
+    wide = cols_loc // parts
     group = 4 if row_devices % 4 == 0 else 1
     half = chips // 2
     last = col_devices - 1
@@ -176,16 +178,11 @@
                     near_ring(NEAR, sn, way, step + 1).start()
                 sib(NEAR, sn, off).start()
 
-    def s_copy(sn, at, way):
-        src = s_buf.at[sn, at]
+    def s_copy(sn, at, way, h, own=False):
+        dst = s_buf.at[sn, at, pl.ds(h * wide, wide)]
         return remote(
-            src, src, s_send.at[sn, at, way], s_recv.at[sn, at], p,
-            q + 1 if way == RIGHT else q - 1,
-        )
-
-    def s_own(sn, way):
-        return remote(
-            s_in.at[sn], s_buf.at[sn, q], s_send.at[sn, q, way], s_recv.at[sn, q], p,
+            s_in.at[sn, pl.ds(h * wide, wide)] if own else dst, dst,
+            s_send.at[sn, at, way, h], s_recv.at[sn, at, h], p,
             q + 1 if way == RIGHT else q - 1,
         )
 
@@ -205,44 +202,47 @@
         return (q >= span(sn)[0]) & (q <= span(sn)[1])
 
     def s_begin(sn):
-        @pl.when(s_up(sn))
-        def _():
-            s_own(sn, RIGHT).start()
-
-        @pl.when(s_down(sn))
-        def _():
-            s_own(sn, LEFT).start()
+        for h in range(parts):
+            @pl.when(s_up(sn))
+            def _():
+                s_copy(sn, q, RIGHT, h, True).start()
+
+            @pl.when(s_down(sn))
+            def _():
+                s_copy(sn, q, LEFT, h, True).start()
 
     def s_sent(sn):
-        @pl.when(s_up(sn))
-        def _():
-            s_own(sn, RIGHT).wait_send()
-
-        @pl.when(s_down(sn))
-        def _():
-            s_own(sn, LEFT).wait_send()
-
-        for dist in range(1, col_devices):
-            @pl.when((q - dist >= 0) & s_here(sn) & s_up(sn))
-            def _():
-                s_copy(sn, q - dist, RIGHT).wait_send()
-
-            @pl.when((q + dist <= last) & s_here(sn) & s_down(sn))
-            def _():
-                s_copy(sn, q + dist, LEFT).wait_send()
+        for h in range(parts):
+            @pl.when(s_up(sn))
+            def _():
+                s_copy(sn, q, RIGHT, h, True).wait_send()
+
+            @pl.when(s_down(sn))
+            def _():
+                s_copy(sn, q, LEFT, h, True).wait_send()
+
+            for dist in range(1, col_devices):
+                @pl.when((q - dist >= 0) & s_here(sn) & s_up(sn))
+                def _():
+                    s_copy(sn, q - dist, RIGHT, h).wait_send()
+
+                @pl.when((q + dist <= last) & s_here(sn) & s_down(sn))
+                def _():
+                    s_copy(sn, q + dist, LEFT, h).wait_send()
 
     def s_step(sn, dist):
-        for way, at, there, onward in (
-            (RIGHT, q - dist, q - dist >= 0, s_up(sn)),
-            (LEFT, q + dist, q + dist <= last, s_down(sn)),
-        ):
-            @pl.when(there & s_here(sn))
-            def _():
-                s_copy(sn, at, way).wait_recv()
-
-                @pl.when(onward)
-                def _():
-                    s_copy(sn, at, way).start()
+        for h in range(parts):
+            for way, at, there, onward in (
+                (RIGHT, q - dist, q - dist >= 0, s_up(sn)),
+                (LEFT, q + dist, q + dist <= last, s_down(sn)),
+            ):
+                @pl.when(there & s_here(sn))
+                def _():
+                    s_copy(sn, at, way, h).wait_recv()
+
+                    @pl.when(onward)
+                    def _():
+                        s_copy(sn, at, way, h).start()
 
     def near(sn, index):
         src = u_in.at[sn] if index == 0 else u_buf.at[panel(OWN, sn), slot(-1)]
@@ -252,27 +252,27 @@
             jnp.where(q == 0, 1, jnp.where(q == last, last - 1, near_q)),
         )
 
-    def o_copy(sn, at, way, src=None):
-        dst = o_all.at[sn, at]
+    def o_copy(sn, at, way, h, src=None):
+        dst = o_all.at[sn, at, pl.ds(h * wide, wide)]
         return remote(
-            dst if src is None else src, dst, o_send.at[sn, at, way], o_recv.at[sn, at], p,
-            q + 1 if way == RIGHT else q - 1,
-        )
-
-    def mine_each(sn, at, remote_do, local_do):
-        for m in range(cols_loc):
+            dst if src is None else src, dst, o_send.at[sn, at, way, h],
+            o_recv.at[sn, at, h], p, q + 1 if way == RIGHT else q - 1,
+        )
+
+    def mine_each(sn, at, h, remote_do, local_do):
+        for m in range(h * wide, (h + 1) * wide):
             v = at + col_devices * m
             to_p = lax.rem(v, row_devices)
             k = v // row_devices
-            if remote_do is not None:
-                @pl.when(to_p != p)
-                def _():
-                    remote_do(
-                        remote(
-                            o_all.at[sn, at, m], o_mine.at[sn, k, p],
-                            mine_send.at[sn, at, m], mine_recv.at[sn, k, p], to_p, q,
-                        )
+
+            @pl.when(to_p != p)
+            def _():
+                remote_do(
+                    remote(
+                        o_all.at[sn, at, m], o_mine.at[sn, k, p],
+                        mine_send.at[sn, at, m], mine_recv.at[sn, k, p], to_p, q,
                     )
+                )
 
             if local_do is not None:
                 @pl.when(to_p == p)
@@ -283,13 +283,16 @@
                         )
                     )
 
-    def hand_out(sn, at):
-        mine_each(sn, at, lambda c: c.start(), lambda c: c.start())
+    def hand_out(sn, at, h):
+        mine_each(sn, at, h, lambda c: c.start(), lambda c: c.start())
 
     def make_o(sn, which, at):
         sib_all(which, sn)
         acc[...] = jnp.zeros_like(acc)
-
+        for h in range(parts):
+            make_part(sn, which, at, h)
+
+    def make_part(sn, which, at, h):
         def add(step, carry):
             first = step * group
             left = jnp.concatenate(
@@ -303,7 +306,7 @@
                 ],
                 axis=1,
             )
-            for m in range(cols_loc):
+            for m in range(h * wide, (h + 1) * wide):
                 right = u_buf[
                     panel(which, sn), pl.ds(first, group), :, m * blk : (m + 1) * blk
                 ].reshape(group * rows, blk)
@@ -313,80 +316,75 @@
             return carry
 
         lax.fori_loop(0, row_devices // group, add, 0)
-        for m in range(cols_loc):
+        for m in range(h * wide, (h + 1) * wide):
             o_stage[sn, which, m] = (-acc[:rows, m * blk : (m + 1) * blk]).astype(o_stage.dtype)
-        stage = o_stage.at[sn, which]
+        stage = o_stage.at[sn, which, pl.ds(h * wide, wide)]
+
         @pl.when(q < last)
         def _():
-            o_copy(sn, at, RIGHT, stage).start()
+            o_copy(sn, at, RIGHT, h, stage).start()
 
         @pl.when(q > 0)
         def _():
-            o_copy(sn, at, LEFT, stage).start()
-
-        keep = pltpu.make_async_copy(stage, o_all.at[sn, at], keep_sem.at[sn, which])
+            o_copy(sn, at, LEFT, h, stage).start()
+
+        keep = pltpu.make_async_copy(
+            stage, o_all.at[sn, at, pl.ds(h * wide, wide)], keep_sem.at[sn, which, h]
+        )
         keep.start()
         keep.wait()
-        hand_out(sn, at)
-
-    def o_step(sn, dist, extra):
+        hand_out(sn, at, h)
+
+    def o_ways(sn, dist, extra):
         for way, origin, there, onward in (
             (RIGHT, q - dist, q - dist >= span(sn)[0], q < last),
             (LEFT, q + dist, q + dist <= span(sn)[1], q > 0),
         ):
             if extra:
                 there = there & ((origin == 1) | (origin == last - 1))
-                at = jnp.where(origin == 1, 0, last)
+                yield way, jnp.where(origin == 1, 0, last), there, onward
             else:
-                at = origin
-            @pl.when(there)
-            def _():
-                o_copy(sn, at, way).wait_recv()
-
-                @pl.when(onward)
-                def _():
-                    o_copy(sn, at, way).start()
-
-                hand_out(sn, at)
+                yield way, origin, there, onward
+
+    def o_step(sn, dist, extra):
+        for h in range(parts):
+            for way, at, there, onward in o_ways(sn, dist, extra):
+                @pl.when(there)
+                def _():
+                    o_copy(sn, at, way, h).wait_recv()
+
+                    @pl.when(onward)
+                    def _():
+                        o_copy(sn, at, way, h).start()
+
+                    hand_out(sn, at, h)
 
     def o_sent(sn):
-        for extra in (False, True) if lent(sn) else (False,):
-            if extra:
-                first = helper
-                at = near_q
-            else:
-                first = s_here(sn)
-                at = q
-
-            @pl.when(first & (q < last))
-            def _():
-                o_copy(sn, at, RIGHT).wait_send()
-
-            @pl.when(first & (q > 0))
-            def _():
-                o_copy(sn, at, LEFT).wait_send()
-
-            @pl.when(first)
-            def _():
-                mine_each(sn, at, lambda c: c.wait_send(), None)
-
-            for dist in range(1, span(sn)[1] + 1):
-                for way, origin, there, onward in (
-                    (RIGHT, q - dist, q - dist >= span(sn)[0], q < last),
-                    (LEFT, q + dist, q + dist <= span(sn)[1], q > 0),
-                ):
-                    if extra:
-                        there = there & ((origin == 1) | (origin == last - 1))
-                        at = jnp.where(origin == 1, 0, last)
-                    else:
-                        at = origin
-                    @pl.when(there & onward)
-                    def _():
-                        o_copy(sn, at, way).wait_send()
-
-                    @pl.when(there)
-                    def _():
-                        mine_each(sn, at, lambda c: c.wait_send(), None)
+        for h in range(parts):
+            for extra in (False, True) if lent(sn) else (False,):
+                first, made = (helper, near_q) if extra else (s_here(sn), q)
+
+                @pl.when(first & (q < last))
+                def _():
+                    o_copy(sn, made, RIGHT, h).wait_send()
+
+                @pl.when(first & (q > 0))
+                def _():
+                    o_copy(sn, made, LEFT, h).wait_send()
+
+                @pl.when(first)
+                def _():
+                    mine_each(sn, made, h, lambda c: c.wait_send(), None)
+
+                for dist in range(1, span(sn)[1] + 1):
+                    for way, at, there, onward in o_ways(sn, dist, extra):
+                        @pl.when(there & onward)
+                        def _():
+                            o_copy(sn, at, way, h).wait_send()
+
+                        @pl.when(there)
+                        def _():
+                            mine_each(sn, at, h, lambda c: c.wait_send(), None)
 
     def make_d(sn):
         acc[...] = jnp.zeros_like(acc)
@@ -397,14 +395,13 @@
                 for i in range(group):
                     here = o_mine.at[sn, k, first + i]
                     pltpu.make_async_copy(here, here, mine_recv.at[sn, k, first + i]).wait()
-                block = o_mine[sn, k, pl.ds(first, group)].reshape(group * rows, blk)
+                block = o_mine[sn, k, pl.ds(first, group)].reshape(group * rows, blk).T
                 for m in range(cols_loc):
                     right = u_buf[
                         panel(OWN, sn), pl.ds(first, group), :, m * blk : (m + 1) * blk
                     ].reshape(group * rows, blk)
-                    acc[k * blk : (k + 1) * blk, m * blk : (m + 1) * blk] += lax.dot_general(
-                        block, right, (((0,), (0,)), ((), ())),
-                        preferred_element_type=jnp.float32,
+                    acc[k * blk : (k + 1) * blk, m * blk : (m + 1) * blk] += jnp.dot(
+                        block, right, preferred_element_type=jnp.float32
                     )
             return carry
 
@@ -444,7 +441,6 @@
                 make_o(sn, NEAR, near_q)
 
     for sn in range(nodes):
-        near_begin(sn, 0)
         s_begin(sn)
     ring_begin(OWN, 0)
     for sn in range(nodes):
@@ -453,12 +449,13 @@
 
     for sn in range(nodes):
         ring_step(OWN, sn, 1)
-        near_begin(sn, 1)
         if sn + 1 < nodes:
             ring_begin(OWN, sn + 1)
         if sn == 0:
             for other in range(nodes):
                 s_step(other, 1)
+            near_begin(0, 0)
+            near_begin(0, 1)
         for step in range(2, half + 1):
             ring_step(OWN, sn, step)
         if sn == 0:
@@ -476,9 +473,9 @@
         o_step(0, dist, False)
     lent_o(0)
     for dist in range(1, col_devices):
+        o_step(0, dist, True)
         for sn in range(1, nodes):
             o_step(sn, dist, False)
-        o_step(0, dist, True)
 
     for sn in range(nodes):
         make_d(sn)
@@ -516,6 +513,7 @@
     u_in = factor_panel.reshape(nodes, rows, panel_cols * blk)
     d_in = diag_inverse.reshape(nodes, panel_cols * blk, diag_cols * blk)
     half = row_devices // 4
+    parts = 2 if panel_cols % 2 == 0 else 1
     dma = pltpu.SemaphoreType.DMA
     bf16 = jnp.bfloat16
     o_all, d_out = pl.pallas_call(
@@ -545,16 +543,16 @@
             dma((2, nodes, 2, half)),
             dma((2, nodes, 2 * half)),
             dma((2, nodes, 2 * half)),
-            dma((nodes, col_devices, 2)),
-            dma((nodes, col_devices)),
+            dma((nodes, col_devices, 2, parts)),
+            dma((nodes, col_devices, parts)),
             dma((nodes, 2)),
             dma((nodes, 2)),
-            dma((nodes, col_devices, 2)),
-            dma((nodes, col_devices)),
+            dma((nodes, col_devices, 2, parts)),
+            dma((nodes, col_devices, parts)),
             dma((nodes, col_devices, panel_cols)),
             dma((nodes, diag_cols, row_devices)),
             dma((2, nodes)),
-            dma((nodes, 2)),
+            dma((nodes, 2, parts)),
         ],
         compiler_params=pltpu.CompilerParams(
             collective_id=0, has_side_effects=True, vmem_limit_bytes=62 * 1024 * 1024

time: 361 us -> 344 us (0.953)
  Pallas kernels: 340 us -> 323 us
    pallas_call x1, Pallas kernels: 340 us -> 323 us  [on_device(): pl.pallas_call(functools.partial(kernel, row_devices, col_devices, rows_l...]
where the time goes in v5:
time: 344 us; the launch traced here: 343 us
  Pallas kernels  323 us (94%)
  local copies, waits for them, and re-layouts  17.1 us (5%)
    pallas_call x1, Pallas kernels, on_device(): pl.pallas_call(functools.partial(kernel, row_devices, col_devices, rows_l...  323 us

profile of v5, /device:TPU:7, one launch (start us, length us, event | category | flops | bytes accessed | tf_op | source)
XLA Modules:
  0.0 343.4 jit_solution(9032380844409408515)
XLA Ops:
  0.6 0.8 copy.14
  1.4 0.1 reshape.33
  1.5 0.1 constant_dynamic-slice_fusion.1
  1.6 0.1 copy.19
  1.7 2.5 broadcast_select_fusion
  4.2 0.0 copy-start
  4.2 1.7 copy.16
  5.9 0.6 copy-done
  6.5 2.7 reshape.35.u_in
  9.2 4.4 %reshape.36.d_in = bf16[2,1024,512]{2,1,0:T(8,128)(2,1)} reshape(bf16[2,4,1,256,2,1,256]{6,4,5,3,2,1,0:T(2,128)(2,1)} %param.6) | data formatting | bytes 4194304 | tf_op jit(solution)/shard_map/reshape | solution.py:514
  13.6 323.1 %shard_map.59 = (bf16[2,4,4,512,256]{4,3,2,1,0:T(8,128)(2,1)}, bf16[2,1024,512]{2,1,0:T(8,128)(2,1)}) custom-call(bf16[2,4,512,256]{3,2,1,0:T(8,128)(2,1)} %bitcast.19, bf16[2,512,1024]{2,1,0:T(8,128)(2,1)} %reshape.35.u_in, bf16[2,1024,512]{2,1,0:T(8,128)(2,1)} %reshape.36.d_in), custom_call_target="tpu_custom_call" | custom-call | flops 17999998976 | bytes 41943040 | tf_op jit(solution)/shard_map/pallas_call | solution.py:519
  336.7 1.7 constant_dynamic-slice_fusion
  338.4 0.0 copy-start.1
  338.4 2.9 copy.17
  341.4 0.0 copy-done.1
  341.4 2.0 reshape.38
  (1 shorter events, 0.0 us)
Async XLA Ops:
  4.2 2.3 copy-start
  338.4 3.0 copy-start.1
